TPU v7x, 32 devices: a whole 2x2x4 slice. The times are simulated.
32 devices in a mesh: dp: 8 (over y, x, core), section: 4 (over z).
Axes of the slice: x: 2, y: 2, z: 4, core: 2. Of those that a mesh axis runs over, the one named last changes fastest.
Arguments:
- tokens: bfloat16 [8192, 768], P(('dp', 'section')), may hold values from -6 to 6
- cotangent: bfloat16 [8192, 768], P(('dp', 'section')), may hold values from -6 to 6
- seg_doc: int32 [32, 2], P('dp'), may hold values from 0 to 1, as said below
- wide_in: bfloat16 [4, 768, 3072], P('section')
- half_out: bfloat16 [4, 1536, 768], P('section'), may hold values from -0.109375 to 0.109375
- norm_gain: float32 [4, 768], P('section'), may hold values from 0.5 to 1.5
- norm_bias: float32 [4, 768], P('section'), may hold values from -1.8 to 1.8
Outputs:
- layer_out: bfloat16 [8192, 768], P(('dp', 'section'))
- tokens_grad: bfloat16 [8192, 768], P(('dp', 'section'))
- wide_in_grad: float32 [4, 768, 3072], P('section')
- half_out_grad: float32 [4, 1536, 768], P('section')
- gain_grad: float32 [4, 768], P('section')
- bias_grad: float32 [4, 768], P('section')
Inputs may be any that keep to these rules, and one draw needn't show every extreme that they name: `seg_doc`: in each row the numbers start at 0 and rise by 0 or 1 from segment to segment. Every group (the 4 rows i with the same i // 4) has a row holding one document of all 2 segments.
All inputs are finite; a program needn't handle non-finite values.
Results may differ from a plain program's by a relative error of at most 0.012.
Values may be sent and summed in bfloat16 or wider, within the bound.
A program may use at most 512 MiB of HBM per device.

v0:
```python
from functools import partial

import jax
import jax.numpy as jnp
from jax import lax
from jax.sharding import PartitionSpec as P

D = 768
HEADS = 12


def passed_along(value, axis, steps):
    count = lax.axis_size(axis)
    leading, last = (max(0, -steps), min(count, count - steps))
    return lax.ppermute(value, axis, [(source, source + steps) for source in range(leading, last)])


def shortened(value):
    return jax.tree.map(lambda a: a.astype(jnp.bfloat16) if a.dtype == jnp.float32 else a, value)


def normalize(summed, gain_row, bias_row):
    average = jnp.mean(summed, axis=-1, keepdims=True)
    centred = summed - average
    inv_dev = lax.rsqrt(jnp.mean(centred * centred, axis=-1, keepdims=True) + 1e-05)
    normed = centred * inv_dev
    return (normed * gain_row + bias_row, normed, inv_dev)


def normalize_backward(grad_out, normed, inv_dev, gain_row):
    grad_full = grad_out.astype(jnp.float32)
    grad_gain = jnp.sum(grad_full * normed, axis=0)
    grad_bias = jnp.sum(grad_full, axis=0)
    grad_normed = grad_full * gain_row
    grad_sum = inv_dev * (
        grad_normed
        - jnp.mean(grad_normed, axis=-1, keepdims=True)
        - normed * jnp.mean(grad_normed * normed, axis=-1, keepdims=True)
    )
    return (grad_sum, grad_gain, grad_bias)


def attention_forward(hidden, weights, gain_row, bias_row, allowed, groups):
    row_count = hidden.shape[0]
    length = row_count // groups
    head_dim = D // HEADS
    qkv_all = jnp.dot(hidden, weights[:, : 3 * D], preferred_element_type=jnp.float32).astype(
        jnp.bfloat16
    )
    split = qkv_all.reshape(groups, length, 3, HEADS, head_dim)
    queries = split[:, :, 0]
    keys_all = split[:, :, 1]
    values = split[:, :, 2]
    scores = jnp.einsum(
        "glhd,gmhd->ghlm", queries, keys_all, preferred_element_type=jnp.float32
    ) * head_dim ** (-0.5)
    if allowed is not None:
        scores = jnp.where(allowed, scores, -1000000000.0)
    attn_probs = jax.nn.softmax(scores, axis=-1)
    probs_low = attn_probs.astype(jnp.bfloat16)
    context = jnp.einsum("ghlm,gmhd->glhd", probs_low, values, preferred_element_type=jnp.float32)
    context = context.reshape(row_count, D).astype(jnp.bfloat16)
    branch = lax.dot_general(
        context, weights[:, 3 * D :], (((1,), (1,)), ((), ())), preferred_element_type=jnp.float32
    )
    output, normed, inv_dev = normalize(hidden.astype(jnp.float32) + branch, gain_row, bias_row)
    return (output, (queries, keys_all, values, attn_probs, probs_low, context, normed, inv_dev))


def attention_backward(hidden, weights, gain_row, saved, grad_out, groups):
    queries, keys_all, values, attn_probs, probs_low, context, normed, inv_dev = saved
    row_count = hidden.shape[0]
    length = row_count // groups
    head_dim = D // HEADS
    scale = head_dim ** (-0.5)
    grad_sum, grad_gain, grad_bias = normalize_backward(grad_out, normed, inv_dev, gain_row)
    grad_branch = grad_sum.astype(jnp.bfloat16)
    grad_wo = lax.dot_general(
        grad_branch, context, (((0,), (0,)), ((), ())), preferred_element_type=jnp.float32
    )
    grad_context = jnp.dot(
        grad_branch, weights[:, 3 * D :], preferred_element_type=jnp.float32
    ).astype(jnp.bfloat16)
    grad_heads = grad_context.reshape(groups, length, HEADS, head_dim)
    grad_probs = jnp.einsum(
        "glhd,gmhd->ghlm", grad_heads, values, preferred_element_type=jnp.float32
    )
    grad_values = jnp.einsum(
        "ghlm,glhd->gmhd", probs_low, grad_heads, preferred_element_type=jnp.float32
    )
    grad_scores = attn_probs * (
        grad_probs - jnp.sum(attn_probs * grad_probs, axis=-1, keepdims=True)
    )
    grad_scores = grad_scores.astype(jnp.bfloat16)
    grad_queries = (
        jnp.einsum("ghlm,gmhd->glhd", grad_scores, keys_all, preferred_element_type=jnp.float32)
        * scale
    )
    grad_keys = (
        jnp.einsum("ghlm,glhd->gmhd", grad_scores, queries, preferred_element_type=jnp.float32)
        * scale
    )
    grad_qkv = (
        jnp.stack([grad_queries, grad_keys, grad_values], axis=2)
        .reshape(row_count, 3 * D)
        .astype(jnp.bfloat16)
    )
    grad_wqkv = lax.dot_general(
        hidden, grad_qkv, (((0,), (0,)), ((), ())), preferred_element_type=jnp.float32
    )
    grad_hidden = (
        lax.dot_general(
            grad_qkv,
            weights[:, : 3 * D],
            (((1,), (1,)), ((), ())),
            preferred_element_type=jnp.float32,
        )
        + grad_sum
    )
    return (grad_hidden, jnp.concatenate([grad_wqkv, grad_wo], axis=1), grad_gain, grad_bias)


def mlp_forward(hidden, w_first, w_second, gain_row, bias_row):
    inner = jnp.dot(hidden, w_first, preferred_element_type=jnp.float32)
    activated = jax.nn.gelu(inner, approximate=False).astype(jnp.bfloat16)
    branch = jnp.dot(activated, w_second, preferred_element_type=jnp.float32)
    output, normed, inv_dev = normalize(hidden.astype(jnp.float32) + branch, gain_row, bias_row)
    return (output, (inner, activated, normed, inv_dev))


def mlp_backward(hidden, w_first, w_second, gain_row, saved, grad_out):
    inner, activated, normed, inv_dev = saved
    grad_sum, grad_gain, grad_bias = normalize_backward(grad_out, normed, inv_dev, gain_row)
    grad_branch = grad_sum.astype(jnp.bfloat16)
    grad_second = lax.dot_general(
        activated, grad_branch, (((0,), (0,)), ((), ())), preferred_element_type=jnp.float32
    )
    grad_act = lax.dot_general(
        grad_branch, w_second, (((1,), (1,)), ((), ())), preferred_element_type=jnp.float32
    )
    unused_out, gelu_pull = jax.vjp(partial(jax.nn.gelu, approximate=False), inner)
    grad_inner = gelu_pull(grad_act)[0].astype(jnp.bfloat16)
    grad_first = lax.dot_general(
        hidden, grad_inner, (((0,), (0,)), ((), ())), preferred_element_type=jnp.float32
    )
    grad_hidden = (
        lax.dot_general(
            grad_inner, w_first, (((1,), (1,)), ((), ())), preferred_element_type=jnp.float32
        )
        + grad_sum
    )
    return (grad_hidden, grad_first, grad_second, grad_gain, grad_bias)


def on_device(tokens, cotangent, seg_doc, wide_in, half_out, norm_gain, norm_bias):
    section_count = lax.axis_size("section")
    section_index = lax.axis_index("section")
    micro_count = seg_doc.shape[0]
    seg_count = seg_doc.shape[1]
    width = tokens.shape[1]
    inputs_all, cotan_all = (
        lax.all_gather(tokens, "section", axis=0, tiled=True),
        lax.all_gather(cotangent, "section", axis=0, tiled=True),
    )
    micro_rows = inputs_all.shape[0] // micro_count
    inputs_all = inputs_all.reshape(micro_count, micro_rows, width)
    cotan_all = cotan_all.reshape(micro_count, micro_rows, width)
    w_local = wide_in[0]
    held_half = half_out[0]
    partner_half = passed_along(held_half, "section", 1)
    w_second = jnp.concatenate([partner_half, held_half], axis=0)
    gain_row = norm_gain[0]
    bias_row = norm_bias[0]
    second_zero = jnp.zeros(w_second.shape, jnp.float32)
    first_zero = jnp.zeros(w_local.shape, jnp.float32)

    def leaders_of(block_rows):
        return block_rows.reshape(seg_count, -1, width)[:, 0]

    def with_leaders(block_rows, leader_rows):
        return (
            block_rows.reshape(seg_count, -1, width)
            .at[:, 0]
            .set(leader_rows)
            .reshape(block_rows.shape)
        )

    def doc_mask(doc_row):
        return (doc_row[:, None] == doc_row[None, :])[None, None]

    def seg_attention(section_in, doc_row):
        return attention_forward(section_in, w_local, gain_row, bias_row, None, seg_count)[
            0
        ].astype(jnp.bfloat16)

    def seg_mlp(section_in, doc_row):
        return mlp_forward(section_in, w_local, w_second, gain_row, bias_row)[0].astype(
            jnp.bfloat16
        )

    def cross_attention_lead(leaders, doc_row):
        return attention_forward(leaders, w_local, gain_row, bias_row, doc_mask(doc_row), 1)[
            0
        ].astype(jnp.bfloat16)

    def cross_mlp_lead(leaders):
        return mlp_forward(leaders, w_local, w_second, gain_row, bias_row)[0].astype(jnp.bfloat16)

    def seg_attention_back(section_in, grad_out, doc_row):
        unused_out, saved = attention_forward(
            section_in, w_local, gain_row, bias_row, None, seg_count
        )
        grad_in, grad_first, grad_gain, grad_bias = attention_backward(
            section_in, w_local, gain_row, saved, grad_out, seg_count
        )
        return (grad_in, grad_first, second_zero, grad_gain, grad_bias)

    def seg_mlp_back(section_in, grad_out, doc_row):
        unused_out, saved = mlp_forward(section_in, w_local, w_second, gain_row, bias_row)
        return mlp_backward(section_in, w_local, w_second, gain_row, saved, grad_out)

    def cross_attention_lead_back(leaders, grad_lead, doc_row):
        unused_out, saved = attention_forward(
            leaders, w_local, gain_row, bias_row, doc_mask(doc_row), 1
        )
        grad_in, grad_first, grad_gain, grad_bias = attention_backward(
            leaders, w_local, gain_row, saved, grad_lead, 1
        )
        return (grad_in, grad_first, second_zero, grad_gain, grad_bias)

    def cross_mlp_lead_back(leaders, grad_lead):
        unused_out, saved = mlp_forward(leaders, w_local, w_second, gain_row, bias_row)
        return mlp_backward(leaders, w_local, w_second, gain_row, saved, grad_lead)

    ticks = micro_count + section_count - 1
    last_section = section_count - 1
    sum_first = first_zero
    sum_second = second_zero
    sum_gain = jnp.zeros_like(gain_row)
    sum_bias = jnp.zeros_like(bias_row)
    input_grads = jnp.zeros((micro_count, micro_rows, width), jnp.bfloat16)
    finished = jnp.zeros((micro_count, micro_rows, width), jnp.bfloat16)

    def cross_attention(section_in, doc_row):
        return with_leaders(section_in, cross_attention_lead(leaders_of(section_in), doc_row))

    def cross_mlp(section_in, doc_row):
        return with_leaders(section_in, cross_mlp_lead(leaders_of(section_in)))

    def spare_forward(section_in, doc_row):
        return jnp.zeros_like(section_in)

    def cross_attention_back(section_in, grad_out, doc_row):
        grad_lead, grad_first, grad_second, grad_gain, grad_bias = cross_attention_lead_back(
            leaders_of(section_in), leaders_of(grad_out), doc_row
        )
        return (
            with_leaders(grad_out.astype(jnp.float32), grad_lead),
            grad_first,
            grad_second,
            grad_gain,
            grad_bias,
        )

    def cross_mlp_back(section_in, grad_out, doc_row):
        grad_lead, grad_first, grad_second, grad_gain, grad_bias = cross_mlp_lead_back(
            leaders_of(section_in), leaders_of(grad_out)
        )
        return (
            with_leaders(grad_out.astype(jnp.float32), grad_lead),
            grad_first,
            grad_second,
            grad_gain,
            grad_bias,
        )

    def spare_backward(section_in, grad_out, doc_row):
        return (
            jnp.zeros(section_in.shape, jnp.float32),
            first_zero,
            second_zero,
            jnp.zeros_like(gain_row),
            jnp.zeros_like(bias_row),
        )

    forward_fns = [seg_attention, seg_mlp, cross_attention, cross_mlp, spare_forward]
    backward_fns = [
        seg_attention_back,
        seg_mlp_back,
        cross_attention_back,
        cross_mlp_back,
        spare_backward,
    ]
    incoming = jnp.zeros((micro_rows, width), jnp.bfloat16)
    kept_inputs = jnp.zeros((micro_count, micro_rows, width), jnp.bfloat16)
    for tick in range(ticks):
        micro = tick - section_index
        active = (micro >= 0) & (micro < micro_count)
        slot = jnp.clip(micro, 0, micro_count - 1)
        section_in = jnp.where(section_index == 0, inputs_all[slot], incoming)
        chosen = jnp.where(active, section_index, section_count)
        section_out = lax.switch(chosen, forward_fns, section_in, seg_doc[slot])
        kept_inputs = kept_inputs.at[slot].set(jnp.where(active, section_in, kept_inputs[slot]))
        finished = finished.at[slot].set(
            jnp.where(active & (section_index == last_section), section_out, finished[slot])
        )
        if tick + 1 < ticks:
            incoming = jax.tree.map(
                lambda part, own: part.astype(own.dtype),
                passed_along(shortened(section_out), "section", 1),
                section_out,
            )
    incoming_grad = jnp.zeros((micro_rows, width), jnp.bfloat16)
    for tick in range(ticks):
        micro = tick - (last_section - section_index)
        active = (micro >= 0) & (micro < micro_count)
        slot = jnp.clip(micro, 0, micro_count - 1)
        grad_out = jnp.where(section_index == last_section, cotan_all[slot], incoming_grad)
        chosen = jnp.where(active, section_index, section_count)
        grad_in, grad_first, grad_second, grad_gain, grad_bias = lax.switch(
            chosen, backward_fns, kept_inputs[slot], grad_out, seg_doc[slot]
        )
        sum_first = sum_first + grad_first
        sum_second = sum_second + grad_second
        sum_gain = sum_gain + grad_gain
        sum_bias = sum_bias + grad_bias
        grad_low = grad_in.astype(jnp.bfloat16)
        input_grads = input_grads.at[slot].set(
            jnp.where(active & (section_index == 0), grad_low, input_grads[slot])
        )
        if tick + 1 < ticks:
            incoming_grad = passed_along(grad_low, "section", -1)
    half_rows = w_second.shape[0] // 2
    odd_section = section_index % 2 == 1
    total_first, total_second, total_gain, total_bias = lax.psum(
        (sum_first, sum_second, sum_gain, sum_bias), "dp"
    )
    passed = passed_along(total_second[:half_rows].astype(jnp.bfloat16), "section", -1).astype(
        jnp.float32
    )
    half_total = jnp.where(odd_section, total_second[half_rows:], passed)
    got_out, got_grad = (
        lax.all_to_all(finished, "section", split_axis=0, concat_axis=0, tiled=True),
        lax.all_to_all(input_grads, "section", split_axis=0, concat_axis=0, tiled=True),
    )
    return (
        got_out[last_section],
        got_grad[0],
        total_first[None],
        half_total[None],
        total_gain[None],
        total_bias[None],
    )


def solution(mesh):
    placed = (
        P(("dp", "section"), None),
        P(("dp", "section"), None),
        P("dp", None),
        P("section", None, None),
        P("section", None, None),
        P("section", None),
        P("section", None),
    )
    return jax.shard_map(
        on_device,
        mesh=mesh,
        in_specs=placed,
        out_specs=(
            P(("dp", "section"), None),
            P(("dp", "section"), None),
            P("section", None, None),
            P("section", None, None),
            P("section", None),
            P("section", None),
        ),
        check_vma=False,
    )
```

profile of v0, /device:TPU:0, one launch (start us, length us, event | category | flops | bytes accessed | tf_op | source)
XLA Modules:
  0.0 1123.8 jit_solution(16636296942766219679)
XLA Ops:
  18.8 52.4 %all-gather.3.cloned.1.call-done = bf16[1024,768]{1,0:T(8,128)(2,1)} async-done(((bf16[256,768]{1,0:T(8,128)(2,1)}), bf16[1024,768]{1,0:T(8,128)(2,1)}) %all-gather.3.cloned.1.call-update) | async-done | bytes 1572880 | tf_op jit(solution)/shard_map/all_gather | solution.py:162
  73.2 24.1 %collective-permute-done = bf16[1536,768]{1,0:T(8,128)(2,1)} collective-permute-done((bf16[1536,768]{1,0:T(8,128)(2,1)}, bf16[1536,768]{1,0:T(8,128)(2,1)}, u32[]{:S(2)}, u32[]{:S(2)}) %collective-permute-start) | collective-permute-done | bytes 2359328 | tf_op jit(solution)/shard_map/ppermute | solution.py:15
  101.5 24.4 %conditional.14 = (bf16[256,768]{1,0:T(8,128)(2,1)}) conditional(s32[]{:T(128)} %clamp.42, (bf16[256,768]{1,0:T(8,128)(2,1)S(1)}, bf16[768,3072]{1,0:T(8,128)(2,1)}, f32[1,768]{1,0:T(1,128)S(1)}, f32[1,768]{1,0:T(1,128)S(1)}) %tuple.1174, (bf16[256,768]{1,0:T(8,128)(2,1)S(1)}, bf16[768,3072]{1,0:T(8,128)(2,1)}, ...), branch_computations={%region_1.6_spmd, %region_6.0_spmd, %region_9.14_spmd, %region_14.... | conditional | flops 2469200128 | bytes 22477868 | solution.py:302
  134.7 29.4 %conditional.15 = (bf16[256,768]{1,0:T(8,128)(2,1)}) conditional(s32[]{:T(128)} %clamp.43, (bf16[256,768]{1,0:T(8,128)(2,1)S(1)}, bf16[768,3072]{1,0:T(8,128)(2,1)}, f32[1,768]{1,0:T(1,128)S(1)}, f32[1,768]{1,0:T(1,128)S(1)}) %tuple.1178, (bf16[256,768]{1,0:T(8,128)(2,1)S(1)}, bf16[768,3072]{1,0:T(8,128)(2,1)}, ...), branch_computations={%region_19.0_spmd, %region_24.27_spmd, %region_27.32_spmd, %region... | conditional | flops 2469200128 | bytes 22477868 | solution.py:302
  171.8 29.2 %conditional.16 = (bf16[256,768]{1,0:T(8,128)(2,1)}) conditional(s32[]{:T(128)} %clamp.44, (bf16[256,768]{1,0:T(8,128)(2,1)S(1)}, bf16[768,3072]{1,0:T(8,128)(2,1)}, f32[1,768]{1,0:T(1,128)S(1)}, f32[1,768]{1,0:T(1,128)S(1)}) %tuple.1182, (bf16[256,768]{1,0:T(8,128)(2,1)S(1)}, bf16[768,3072]{1,0:T(8,128)(2,1)}, ...), branch_computations={%region_37.42_spmd, %region_42.45_spmd, %region_45.50_spmd, %regio... | conditional | flops 2469200128 | bytes 22477868 | solution.py:302
  208.8 29.4 %conditional.17 = (bf16[256,768]{1,0:T(8,128)(2,1)}) conditional(s32[]{:T(128)} %clamp.45, (bf16[256,768]{1,0:T(8,128)(2,1)S(1)}, bf16[768,3072]{1,0:T(8,128)(2,1)}, f32[1,768]{1,0:T(1,128)S(1)}, f32[1,768]{1,0:T(1,128)S(1)}) %tuple.1188, (bf16[256,768]{1,0:T(8,128)(2,1)S(1)}, bf16[768,3072]{1,0:T(8,128)(2,1)}, ...), branch_computations={%region_55.60_spmd, %region_60.63_spmd, %region_63.68_spmd, %regio... | conditional | flops 2469200128 | bytes 22477868 | solution.py:302
  253.0 14.8 %collective-permute-start.5 = (bf16[256,768]{1,0:T(8,128)(2,1)}, bf16[256,768]{1,0:T(8,128)(2,1)S(1)}, u32[]{:S(2)}, u32[]{:S(2)}) collective-permute-start(bf16[256,768]{1,0:T(8,128)(2,1)} %get-tuple-element.2655), channel_id=1, source_target_pairs={{0,1},{1,2},{2,3},{4,5},{5,6},{6,7},{8,9},{9,10},{10,11},{12,13},{... | collective-permute-start | bytes 1179656 | tf_op jit(solution)/shard_map/ppermute | solution.py:15
  291.8 19.0 %conditional.21 = (f32[3072,768]{1,0:T(8,128)}, f32[768]{0:T(1024)S(1)}, f32[768]{0:T(1024)S(1)}, bf16[256,768]{1,0:T(8,128)(2,1)S(1)}, f32[768,3072]{1,0:T(8,128)}) conditional(s32[]{:T(128)} %clamp.49, (bf16[768,3072]{1,0:T(8,128)(2,1)}, bf16[256,768]{1,0:T(8,128)(2,1)S(1)}, bf16[256,768]{1,0:T(8,128)(2,1)S(1)}, ...), branch_computations={%region_127.137_spmd, %region_137.144_spmd, %region_144.154_spmd, ... | conditional | flops 7318535168 | bytes 145686912 | solution.py:320
  312.1 22.0 %collective-permute-done.7 = bf16[256,768]{1,0:T(8,128)(2,1)S(1)} collective-permute-done((bf16[256,768]{1,0:T(8,128)(2,1)S(1)}, bf16[256,768]{1,0:T(8,128)(2,1)S(1)}, u32[]{:S(2)}, u32[]{:S(2)}) %collective-permute-start.7) | collective-permute-done | bytes 393248 | tf_op jit(solution)/shard_map/ppermute | solution.py:15
  335.2 20.1 %conditional.22 = (f32[3072,768]{1,0:T(8,128)}, f32[768]{0:T(1024)S(1)}, f32[768]{0:T(1024)}, bf16[256,768]{1,0:T(8,128)(2,1)}, f32[768,3072]{1,0:T(8,128)}) conditional(s32[]{:T(128)} %clamp.50, (bf16[768,3072]{1,0:T(8,128)(2,1)}, bf16[256,768]{1,0:T(8,128)(2,1)}, bf16[256,768]{1,0:T(8,128)(2,1)S(1)}, ...), branch_computations={%region_163.173_spmd, %region_173.180_spmd, %region_180.190_spmd, ... | conditional | flops 7318535168 | bytes 152052384 | solution.py:320
  366.6 19.9 %conditional.23 = (f32[3072,768]{1,0:T(8,128)}, f32[768]{0:T(1024)S(1)}, f32[768]{0:T(1024)}, bf16[256,768]{1,0:T(8,128)(2,1)}, f32[768,3072]{1,0:T(8,128)}) conditional(s32[]{:T(128)} %clamp.51, (bf16[768,3072]{1,0:T(8,128)(2,1)}, bf16[256,768]{1,0:T(8,128)(2,1)S(1)}, bf16[256,768]{1,0:T(8,128)(2,1)S(1)}, ...), branch_computations={%region_199.209_spmd, %region_209.216_spmd, %region_216.226_spmd, ... | conditional | flops 7318535168 | bytes 147333696 | solution.py:320
  387.8 79.6 %collective-permute-done.9 = bf16[256,768]{1,0:T(8,128)(2,1)S(1)} collective-permute-done((bf16[256,768]{1,0:T(8,128)(2,1)}, bf16[256,768]{1,0:T(8,128)(2,1)S(1)}, u32[]{:S(2)}, u32[]{:S(2)}) %collective-permute-start.9) | collective-permute-done | bytes 393248 | tf_op jit(solution)/shard_map/ppermute | solution.py:15
  468.4 70.0 %conditional.24 = (f32[3072,768]{1,0:T(8,128)}, f32[768]{0:T(1024)S(1)}, f32[768]{0:T(1024)}, bf16[256,768]{1,0:T(8,128)(2,1)}, f32[768,3072]{1,0:T(8,128)}) conditional(s32[]{:T(128)} %clamp.52, (bf16[768,3072]{1,0:T(8,128)(2,1)}, bf16[256,768]{1,0:T(8,128)(2,1)}, bf16[256,768]{1,0:T(8,128)(2,1)S(1)}, ...), branch_computations={%region_235.245_spmd, %region_245.252_spmd, %region_252.262_spmd, ... | conditional | flops 7318535168 | bytes 152052384 | solution.py:320
  471.7 9.6 copy.391
  514.7 9.7 copy.595
  549.4 60.1 %conditional.25 = (f32[3072,768]{1,0:T(8,128)}, f32[768]{0:T(1024)S(1)}, f32[768]{0:T(1024)}, bf16[256,768]{1,0:T(8,128)(2,1)}, f32[768,3072]{1,0:T(8,128)}) conditional(s32[]{:T(128)} %clamp.53, (bf16[768,3072]{1,0:T(8,128)(2,1)}, bf16[256,768]{1,0:T(8,128)(2,1)S(1)}, bf16[256,768]{1,0:T(8,128)(2,1)S(1)}, ...), branch_computations={%region_271.281_spmd, %region_281.288_spmd, %region_288.298_spmd, ... | conditional | flops 7318535168 | bytes 147333696 | solution.py:320
  585.8 9.7 copy.600
  620.5 61.1 %conditional.26 = (f32[3072,768]{1,0:T(8,128)}, f32[768]{0:T(1024)S(1)}, f32[768]{0:T(1024)}, bf16[256,768]{1,0:T(8,128)(2,1)}, f32[768,3072]{1,0:T(8,128)}) conditional(s32[]{:T(128)} %clamp.54, (bf16[768,3072]{1,0:T(8,128)(2,1)}, bf16[256,768]{1,0:T(8,128)(2,1)}, bf16[256,768]{1,0:T(8,128)(2,1)S(1)}, ...), branch_computations={%region_307.317_spmd, %region_317.324_spmd, %region_324.334_spmd, ... | conditional | flops 7318535168 | bytes 152052384 | solution.py:320
  692.6 65.7 %conditional.27 = (f32[3072,768]{1,0:T(8,128)}, f32[768]{0:T(1024)S(1)}, f32[768]{0:T(1024)}, bf16[256,768]{1,0:T(8,128)(2,1)S(1)}, f32[768,3072]{1,0:T(8,128)}) conditional(s32[]{:T(128)} %clamp.55, (bf16[768,3072]{1,0:T(8,128)(2,1)}, bf16[256,768]{1,0:T(8,128)(2,1)S(1)}, bf16[256,768]{1,0:T(8,128)(2,1)S(1)}, ...), branch_computations={%region_343.353_spmd, %region_353.360_spmd, %region_360.370_spmd, ... | conditional | flops 7318535168 | bytes 137896480 | solution.py:320
  758.2 25.4 %add_add_fusion = f32[3072,768]{1,0:T(8,128)} fusion(f32[3072,768]{1,0:T(8,128)} %get-tuple-element.1734, f32[3072,768]{1,0:T(8,128)} %get-tuple-element.1733, f32[3072,768]{1,0:T(8,128)} %get-tuple-element.1732, f32[3072,768]{1,0:T(8,128)} %get-tuple-element.1731, f32[3072,768]{1,0:T(8,128)} %get-tuple-element.1730, f32[3072,768]{1,0:T(8,128)} %get-tuple-element.1728, ...), kind=kLoop, calls=%fused_computation.2730 | loop fusion | flops 14155776 | bytes 75497472 | tf_op jit(solution)/shard_map/add | solution.py:324
  783.6 26.7 %add_bitcast_fusion = f32[1,768,3072]{2,1,0:T(8,128)} fusion(f32[768,3072]{1,0:T(8,128)} %get-tuple-element.1923, f32[768,3072]{1,0:T(8,128)} %get-tuple-element.1922, f32[768,3072]{1,0:T(8,128)} %get-tuple-element.1921, f32[768,3072]{1,0:T(8,128)} %get-tuple-element.1920, f32[768,3072]{1,0:T(8,128)} %get-tuple-element.1919, ...), kind=kLoop, calls=%fused_computation.2731 | loop fusion | flops 14155776 | bytes 75497472 | tf_op jit(solution)/shard_map/broadcast_in_dim | solution.py:349
  849.3 199.2 %all-reduce.4.cloned.1.call-done = (f32[1,768,3072]{2,1,0:T(8,128)}, f32[3072,768]{1,0:T(8,128)}) async-done(((f32[1,768,3072]{2,1,0:T(8,128)}, f32[3072,768]{1,0:T(8,128)}), (f32[1,768,3072]{2,1,0:T(8,128)}, f32[3072,768]{1,0:T(8,128)})) %all-reduce.4.cloned.1.call-update) | async-done | bytes 18874384 | tf_op jit(solution)/shard_map/psum | solution.py:335
  1054.7 13.7 %all-reduce = (f32[1,768]{1,0:T(1,128)}, f32[1,768]{1,0:T(1,128)}) all-reduce(f32[1,768]{1,0:T(1,128)S(1)} %broadcast_in_dim.346, f32[1,768]{1,0:T(1,128)S(1)} %broadcast_in_dim.356), channel_id=1, replica_groups=mesh['dp'=8,'section'=4] {'dp'}, use_global_device_ids=true, to_apply=%region_380.381 | all-reduce | flops 1536 | bytes 12288 | tf_op jit(solution)/shard_map/psum | solution.py:335
  1069.2 38.4 %collective-permute-done.13 = bf16[1536,768]{1,0:T(8,128)(2,1)} collective-permute-done((bf16[1536,768]{1,0:T(8,128)(2,1)}, bf16[1536,768]{1,0:T(8,128)(2,1)}, u32[]{:S(2)}, u32[]{:S(2)}) %collective-permute-start.13) | collective-permute-done | bytes 2359328 | tf_op jit(solution)/shard_map/ppermute | solution.py:15
  (541 shorter events, 483.2 us)
Async XLA Ops:
  7.2 64.1 %all-gather.3.cloned.1.call-start = ((), (), s32[]{:S(2)}) async-start(), calls=%async_computation.2 | async-start | bytes 1966080 | tf_op jit(solution)/shard_map/all_gather | solution.py:162
  7.9 119.4 %all-gather.5.cloned.1.call-start = ((), (), s32[]{:S(2)}) async-start(), calls=%async_computation.3 | async-start | bytes 1966080 | tf_op jit(solution)/shard_map/all_gather | solution.py:163
  7.9 89.4 %collective-permute-start = (bf16[1536,768]{1,0:T(8,128)(2,1)}, bf16[1536,768]{1,0:T(8,128)(2,1)}, u32[]{:S(2)}, u32[]{:S(2)}) collective-permute-start(bf16[1536,768]{1,0:T(8,128)(2,1)} %bitcast.2617), channel_id=1, source_target_pairs={{0,1},{1,2},{2,3},{4,5},{5,6},{6,7},{8,9},{9,10},{10,11},{12,13},{... | collective-permute-start | bytes 7077896 | tf_op jit(solution)/shard_map/ppermute | solution.py:15
  14.3 1034.1 %all-reduce.4.cloned.1.call-start = ((), (), s32[]{:S(2)}) async-start(), calls=%async_computation.4 | async-start | bytes 37748736 | tf_op jit(solution)/shard_map/psum | solution.py:335
  125.9 7.2 collective-permute-start.1
  164.0 6.9 collective-permute-start.2
  201.0 6.9 collective-permute-start.3
  238.2 6.9 collective-permute-start.4
  253.0 20.3 %collective-permute-start.5 = (bf16[256,768]{1,0:T(8,128)(2,1)}, bf16[256,768]{1,0:T(8,128)(2,1)S(1)}, u32[]{:S(2)}, u32[]{:S(2)}) collective-permute-start(bf16[256,768]{1,0:T(8,128)(2,1)} %get-tuple-element.2655), channel_id=1, source_target_pairs={{0,1},{1,2},{2,3},{4,5},{5,6},{6,7},{8,9},{9,10},{10,11},{12,13},{... | collective-permute-start | bytes 1179656 | tf_op jit(solution)/shard_map/ppermute | solution.py:15
  278.9 9.9 collective-permute-start.6
  310.8 23.3 %collective-permute-start.7 = (bf16[256,768]{1,0:T(8,128)(2,1)S(1)}, bf16[256,768]{1,0:T(8,128)(2,1)S(1)}, u32[]{:S(2)}, u32[]{:S(2)}) collective-permute-start(bf16[256,768]{1,0:T(8,128)(2,1)S(1)} %get-tuple-element.1714), channel_id=1, source_target_pairs={{1,0},{2,1},{3,2},{5,4},{6,5},{7,6},{9,8},{10,9},{11,10},{13,12},{... | collective-permute-start | bytes 1179656 | tf_op jit(solution)/shard_map/ppermute | solution.py:15
  355.3 10.2 collective-permute-start.8
  386.5 80.9 %collective-permute-start.9 = (bf16[256,768]{1,0:T(8,128)(2,1)}, bf16[256,768]{1,0:T(8,128)(2,1)S(1)}, u32[]{:S(2)}, u32[]{:S(2)}) collective-permute-start(bf16[256,768]{1,0:T(8,128)(2,1)} %get-tuple-element.1716), channel_id=1, source_target_pairs={{1,0},{2,1},{3,2},{5,4},{6,5},{7,6},{9,8},{10,9},{11,10},{13,12},{... | collective-permute-start | bytes 1179656 | tf_op jit(solution)/shard_map/ppermute | solution.py:15
  538.5 9.9 collective-permute-start.10
  609.6 9.9 collective-permute-start.11
  681.6 9.9 collective-permute-start.12
  817.9 27.7 %all-to-all-start = ((bf16[4,256,768]{2,1,0:T(8,128)(2,1)}), bf16[4,256,768]{2,1,0:T(8,128)(2,1)S(1)}, u32[]{:S(2)}, u32[]{:S(2)}) async-start(bf16[4,256,768]{2,1,0:T(8,128)(2,1)} %fusion.1889), calls=%async_computation | async-start | bytes 3145728 | tf_op jit(solution)/shard_map/all_to_all | solution.py:343
  845.5 222.8 %all-to-all-start.1 = ((bf16[4,256,768]{2,1,0:T(8,128)(2,1)}), bf16[4,256,768]{2,1,0:T(8,128)(2,1)S(1)}, u32[]{:S(2)}, u32[]{:S(2)}) async-start(bf16[4,256,768]{2,1,0:T(8,128)(2,1)} %fusion.1877), calls=%async_computation.1 | async-start | bytes 3145728 | tf_op jit(solution)/shard_map/all_to_all | solution.py:344
  849.2 205.4 %copy-start.115 = (f32[768]{0:T(1024)S(1)}, f32[768]{0:T(1024)}, u32[]{:S(2)}) copy-start(f32[768]{0:T(1024)} %copy-done.114) | copy-start | bytes 9220
  849.2 205.4 %copy-start.119 = (f32[768]{0:T(1024)S(1)}, f32[768]{0:T(1024)}, u32[]{:S(2)}) copy-start(f32[768]{0:T(1024)} %copy-done.118) | copy-start | bytes 9220
  849.2 205.4 %copy-start.122 = (f32[768]{0:T(1024)S(1)}, f32[768]{0:T(1024)}, u32[]{:S(2)}) copy-start(f32[768]{0:T(1024)} %copy-done.121) | copy-start | bytes 9220
  849.2 205.4 %copy-start.125 = (f32[768]{0:T(1024)S(1)}, f32[768]{0:T(1024)}, u32[]{:S(2)}) copy-start(f32[768]{0:T(1024)} %copy-done.124) | copy-start | bytes 9220
  849.2 205.4 %copy-start.128 = (f32[768]{0:T(1024)S(1)}, f32[768]{0:T(1024)}, u32[]{:S(2)}) copy-start(f32[768]{0:T(1024)} %copy-done.127) | copy-start | bytes 9220
  1052.4 55.1 %collective-permute-start.13 = (bf16[1536,768]{1,0:T(8,128)(2,1)}, bf16[1536,768]{1,0:T(8,128)(2,1)}, u32[]{:S(2)}, u32[]{:S(2)}) collective-permute-start(bf16[1536,768]{1,0:T(8,128)(2,1)} %slice.2029), channel_id=1, source_target_pairs={{1,0},{2,1},{3,2},{5,4},{6,5},{7,6},{9,8},{10,9},{11,10},{13,12},{... | collective-permute-start | bytes 7077896 | tf_op jit(solution)/shard_map/ppermute | solution.py:15
  (118 other events, 2447.0 us)
Sparse Core Ops, SparseCore 0:
  9.6 61.6 all-gather.2
  72.8 41.7 all-gather.4
  810.5 237.9 all-reduce.3
where the time goes:
time: 1130 us; the launch traced here: 1120 us
  waiting for transfers between devices  471 us (42%)
  local copies, waits for them, and re-layouts  179 us (16%)
  other arithmetic  148 us (13%)
  matrix products  133 us (12%)
  loops' own time  117 us (10%)
  starting transfers between devices  47.2 us (4%)
  between operations  15.1 us (1%)
  blocking collectives  13.7 us (1%)
    ppermute x14, waiting for transfers between devices, passed_along(): lax.ppermute(value, axis, [(source, source + steps) for source in range(l...  213 us
    psum x1, waiting for transfers between devices, on_device(): lax.psum((sum_first, sum_second, sum_gain, sum_bias), 'dp')  199 us
    another operation x7, loops' own time, on_device(): lax.switch(chosen, backward_fns, kept_inputs[slot], grad_out, seg_doc[slot])  75.6 us
    all_gather x1, waiting for transfers between devices, on_device(): lax.all_gather(tokens, 'section', axis=0, tiled=True)  52.4 us
    another operation x7, loops' own time, on_device(): section_out = lax.switch(chosen, forward_fns, section_in, seg_doc[slot])  41.1 us
    ppermute x14, starting transfers between devices, passed_along(): lax.ppermute(value, axis, [(source, source + steps) for source in range(l...  39.8 us
    cond x4, local copies, waits for them, and re-layouts, on_device(): lax.switch(chosen, backward_fns, kept_inputs[slot], grad_out, seg_doc[slot])  38.4 us
    concatenate x4, other arithmetic, attention_backward(): jnp.concatenate([grad_wqkv, grad_wo], axis=1)  30.1 us
  transfers between devices with their start and end apart: 19, of which 17 were waited for; matrix products, arithmetic and copies ran while one was open for 7% of the time, Pallas kernels for 0%

commit v1 on v0

v1 whole, which is shorter than its diff:
```python
from functools import partial

import jax
import jax.numpy as jnp
from jax import lax
from jax.experimental import pallas as pl
from jax.experimental.pallas import tpu as pltpu
from jax.sharding import PartitionSpec as P

D = 768
HEADS = 12
CUBE = 8
PIECE = D // CUBE
HALF = PIECE // 2
HOLDER = (0, 0, 0, 0, 1, 1, 1, 1, 0, 0, 1, 1, 2, 2)
GATHERED = len(HOLDER)
REDUCED = 12
OWN = {0: (0, 1, 2, 3, 8, 9), 1: (4, 5, 6, 7, 10, 11)}
PACK = 2 * D + 4 * D + 2 * D + D


def position():
    index = lax.axis_index("dp")
    return (lax.rem(index // 4, 2), lax.rem(index // 2, 2), lax.rem(index, 2), index // CUBE)


def cube_peer(y, x, core, group):
    return {"dp": group * CUBE + y * 4 + x * 2 + core}


def greet(partners):
    barrier = pltpu.get_barrier_semaphore()
    for partner in partners:
        pl.semaphore_signal(
            barrier, inc=1, device_id=partner, device_id_type=pl.DeviceIdType.MESH
        )
    return barrier


def remote(source, target, send, receive, device):
    return pltpu.make_async_remote_copy(
        src_ref=source,
        dst_ref=target,
        send_sem=send,
        recv_sem=receive,
        device_id=device,
        device_id_type=pl.DeviceIdType.MESH,
    )


def gather_kernel(
    sections, order, wide, half, vector, full, vectors,
    line_send, line_recv, cube_send, cube_recv, vector_send, vector_recv, local_sem,
):
    me = lax.axis_index("section")
    y, x, core, group = position()
    beside_x = cube_peer(y, 1 - x, core, group)
    beside_y = cube_peer(1 - y, x, core, group)
    beside_core = cube_peer(y, x, 1 - core, group)
    others = [{"section": lax.rem(me + step, sections)} for step in range(1, sections)]
    barrier = greet([beside_x, beside_y, beside_core] + others)
    pl.semaphore_wait(barrier, sections + 2)

    row = ((y * 2 + x) * 2 + core) * PIECE

    def held(block, first, rows):
        if block < 8:
            return wide.at[pl.ds(first, rows), pl.ds((block % 4) * D, D)]
        return half.at[pl.ds((block % 2) * D + first, rows), :]

    def line_copy(block, step, from_holder):
        piece = full.at[block, y, x, core]
        source = held(block, pl.multiple_of(row, PIECE), PIECE) if from_holder else piece
        return remote(
            source,
            piece,
            line_send.at[block, 0 if step > 0 else 1],
            line_recv.at[block],
            {"section": lax.rem(me + step + sections, sections)},
        )

    def local_copy(block, part):
        yy, xx, cc = part // 4, part // 2 % 2, part % 2
        return pltpu.make_async_copy(
            held(block, part * PIECE, PIECE), full.at[block, yy, xx, cc], local_sem.at[block, part]
        )

    vector_copies = [
        remote(
            vector, vectors.at[me], vector_send.at[step], vector_recv.at[step], others[step - 1]
        )
        for step in range(1, sections)
    ]
    for copy in vector_copies:
        copy.start()
    own_vector = pltpu.make_async_copy(vector, vectors.at[me], vector_send.at[0])
    own_vector.start()

    def cube_copies(block):
        upper, lower = pl.ds(0, HALF), pl.ds(HALF, HALF)
        parts = [
            (full.at[block, y, x, core, upper], beside_x),
            (full.at[block, y, x, core, lower], beside_y),
            (full.at[block, y, :, core, upper], beside_y),
            (full.at[block, :, x, core, lower], beside_x),
            (full.at[block, :, :, core], beside_core),
        ]
        return [
            partial(remote, ref, ref, cube_send.at[block, i], cube_recv.at[block, i], peer)
            for i, (ref, peer) in enumerate(parts)
        ]

    def gets(block):
        return me > HOLDER[block] if block >= REDUCED else me != HOLDER[block]

    def stage_line(block):
        holder = HOLDER[block]

        @pl.when(me == holder)
        def _():
            line_copy(block, 1, True).start()
            if holder > 0 and block < REDUCED:
                line_copy(block, -1, True).start()
            if block < REDUCED:
                for part in range(CUBE):
                    local_copy(block, part).start()

        @pl.when(me > holder)
        def _():
            copy = line_copy(block, 1, False)
            copy.wait_recv()

            @pl.when(me < sections - 1)
            def _():
                copy.start()

        if holder > 0 and block < REDUCED:

            @pl.when(me < holder)
            def _():
                copy = line_copy(block, -1, False)
                copy.wait_recv()

                @pl.when(me > 0)
                def _():
                    copy.start()

    def stage_one(block):
        @pl.when(gets(block))
        def _():
            copies = cube_copies(block)
            copies[0]().start()
            copies[1]().start()

    def stage_two(block):
        @pl.when(gets(block))
        def _():
            copies = cube_copies(block)
            copies[0]().wait_recv()
            copies[2]().start()
            copies[1]().wait_recv()
            copies[3]().start()

    def stage_three(block):
        @pl.when(gets(block))
        def _():
            copies = cube_copies(block)
            copies[2]().wait_recv()
            copies[3]().wait_recv()
            copies[4]().start()

    def finish(block):
        holder = HOLDER[block]

        @pl.when(gets(block))
        def _():
            copies = cube_copies(block)
            copies[4]().wait_recv()
            for copy in copies:
                copy().wait_send()

        @pl.when(me == holder)
        def _():
            line_copy(block, 1, True).wait_send()
            if holder > 0 and block < REDUCED:
                line_copy(block, -1, True).wait_send()
            if block < REDUCED:
                for part in range(CUBE):
                    local_copy(block, part).wait()

        @pl.when((me > holder) & (me < sections - 1))
        def _():
            line_copy(block, 1, False).wait_send()

        if holder > 1 and block < REDUCED:

            @pl.when((me < holder) & (me > 0))
            def _():
                line_copy(block, -1, False).wait_send()

    stages = (stage_line, stage_one, stage_two, stage_three)
    for tick in range(len(order) + len(stages) - 1):
        for place, stage in enumerate(stages):
            if 0 <= tick - place < len(order):
                stage(order[tick - place])
    for block in order:
        finish(block)
    own_vector.wait()
    for copy in vector_copies:
        copy.wait()


def gather_weights(sections, wide, half, vector):
    order = (0, 1, 2, 4, 3, 5, 6, 7, 8, 10, 9, 11, 12, 13)
    full, vectors = pl.pallas_call(
        partial(gather_kernel, sections, order),
        out_shape=(
            jax.ShapeDtypeStruct((GATHERED, 2, 2, 2, PIECE, D), jnp.bfloat16),
            jax.ShapeDtypeStruct((sections,) + vector.shape, jnp.float32),
        ),
        in_specs=[pl.BlockSpec(memory_space=pl.ANY)] * 3,
        out_specs=[pl.BlockSpec(memory_space=pl.ANY)] * 2,
        scratch_shapes=[
            pltpu.SemaphoreType.DMA((GATHERED, 2)),
            pltpu.SemaphoreType.DMA((GATHERED,)),
            pltpu.SemaphoreType.DMA((GATHERED, 5)),
            pltpu.SemaphoreType.DMA((GATHERED, 5)),
            pltpu.SemaphoreType.DMA((sections,)),
            pltpu.SemaphoreType.DMA((sections,)),
            pltpu.SemaphoreType.DMA((GATHERED, CUBE)),
        ],
        compiler_params=pltpu.CompilerParams(collective_id=0, has_side_effects=True),
    )(wide, half, vector)
    return full.reshape(GATHERED, D, D), vectors


def reduce_kernel(
    sections, replicas, order, parts, pack, small, total, packs, smalls,
    core_in, running, one_a, one_b, two_a, two_b, line_in, group_in, small_all, small_sum,
    load_sem, rs_send, rs_recv, line_send, line_recv, group_send, group_recv,
    ag_send, ag_recv, own_sem, pack_send, pack_recv, small_send, small_recv, sum_send, sum_recv,
):
    me = lax.axis_index("section")
    index = lax.axis_index("dp")
    y, x, core, group = position()
    groups = replicas // CUBE
    beside_x = cube_peer(y, 1 - x, core, group)
    beside_y = cube_peer(1 - y, x, core, group)
    beside_core = cube_peer(y, x, 1 - core, group)
    others = [{"section": lax.rem(me + step, sections)} for step in range(1, sections)]
    barrier = greet(others)

    def replica(step):
        return {"dp": lax.rem(index + step, replicas)}

    @pl.loop(1, replicas)
    def _(step):
        pl.semaphore_signal(
            barrier, inc=1, device_id=replica(step), device_id_type=pl.DeviceIdType.MESH
        )

    pl.semaphore_wait(barrier, sections - 1 + replicas - 1)

    upper, lower = pl.ds(0, HALF), pl.ds(HALF, HALF)

    def add(target, *sources):
        value = target[...].astype(jnp.float32)
        for source in sources:
            value = value + source[...].astype(jnp.float32)
        target[...] = value.astype(jnp.bfloat16)

    def small_copy(step):
        return remote(
            small, small_all.at[index], small_send.at[step], small_recv.at[step], replica(step)
        )

    def pack_copy(step):
        return remote(
            pack, packs.at[index], pack_send.at[step], pack_recv.at[step], replica(step)
        )

    @pl.loop(1, replicas)
    def _(step):
        small_copy(step).start()

    own_small = pltpu.make_async_copy(small, small_all.at[index], small_send.at[0])
    own_small.start()
    own_pack = pltpu.make_async_copy(pack, packs.at[index], pack_send.at[0])
    own_pack.start()

    def load(block):
        return pltpu.make_async_copy(
            parts.at[block, :, :, core], running.at[block], load_sem.at[block]
        )

    def scatter(block):
        run = running.at[block]
        pairs = [
            (parts.at[block, :, :, 1 - core], core_in.at[block], beside_core),
            (run.at[:, 1 - x, upper], one_a.at[block], beside_x),
            (run.at[1 - y, :, lower], one_b.at[block], beside_y),
            (run.at[1 - y, x, upper], two_a.at[block], beside_y),
            (run.at[y, 1 - x, lower], two_b.at[block], beside_x),
        ]
        return [
            partial(remote, source, target, rs_send.at[block, i], rs_recv.at[block, i], peer)
            for i, (source, target, peer) in enumerate(pairs)
        ]

    def to_line(block, step):
        return remote(
            running.at[block, y, x],
            line_in.at[block, 0 if step < 0 else 1],
            line_send.at[block],
            line_recv.at[block, 0 if step < 0 else 1],
            {"section": lax.rem(me + step + sections, sections)},
        )

    def to_group(block, step):
        return remote(
            running.at[block, y, x],
            group_in.at[block, step - 1],
            group_send.at[block, step - 1],
            group_recv.at[block, step - 1],
            {"dp": lax.rem(index + step * CUBE, replicas)},
        )

    def gather(block):
        place = OWN[HOLDER[block]].index(block)
        out = total.at[place]
        pairs = [
            (running.at[block, y, x, upper], out.at[y, x, core, upper], beside_y),
            (running.at[block, y, x, lower], out.at[y, x, core, lower], beside_x),
            (out.at[:, x, core, upper], out.at[:, x, core, upper], beside_x),
            (out.at[y, :, core, lower], out.at[y, :, core, lower], beside_y),
            (out.at[:, :, core], out.at[:, :, core], beside_core),
        ]
        return [
            partial(remote, source, target, ag_send.at[place, i], ag_recv.at[place, i], peer)
            for i, (source, target, peer) in enumerate(pairs)
        ]

    def own_piece(block):
        place = OWN[HOLDER[block]].index(block)
        return pltpu.make_async_copy(
            running.at[block, y, x], total.at[place, y, x, core], own_sem.at[place]
        )

    def stage_core(block):
        scatter(block)[0]().start()
        load(block).start()

    def stage_one(block):
        copies = scatter(block)
        load(block).wait()
        copies[0]().wait_recv()
        for yy in range(2):
            for xx in range(2):
                add(running.at[block, yy, xx], core_in.at[block, yy, xx])
        copies[1]().start()
        copies[2]().start()

    def stage_two(block):
        copies = scatter(block)
        copies[1]().wait_recv()
        for yy in range(2):
            add(running.at[block, yy, x, upper], one_a.at[block, yy])
        copies[3]().start()
        copies[2]().wait_recv()
        for xx in range(2):
            add(running.at[block, y, xx, lower], one_b.at[block, xx])
        copies[4]().start()

    def stage_three(block):
        copies = scatter(block)
        copies[3]().wait_recv()
        add(running.at[block, y, x, upper], two_a.at[block])
        copies[4]().wait_recv()
        add(running.at[block, y, x, lower], two_b.at[block])
        if groups > 1:
            for step in range(1, groups):
                to_group(block, step).start()
            for step in range(1, groups):
                to_group(block, step).wait()
            for step in range(1, groups):
                add(running.at[block, y, x], group_in.at[block, step - 1])

    def stage_line(hop, block):
        holder = HOLDER[block]
        for section in range(sections):
            distance = abs(section - holder)
            from_above = sections - 1 - section if section >= holder else -1
            from_below = section if section <= holder else -1
            if max(from_above, from_below) != hop:
                continue

            @pl.when(me == section)
            def _():
                if from_above > 0:
                    to_line(block, -1).wait_recv()
                    add(running.at[block, y, x], line_in.at[block, 0])
                if from_below > 0:
                    to_line(block, 1).wait_recv()
                    add(running.at[block, y, x], line_in.at[block, 1])
                if distance > 0:
                    to_line(block, -1 if section > holder else 1).start()

    def stage_spread(block):
        @pl.when(me == HOLDER[block])
        def _():
            copies = gather(block)
            own_piece(block).start()
            copies[0]().start()
            copies[1]().start()

    def stage_spread_two(block):
        @pl.when(me == HOLDER[block])
        def _():
            copies = gather(block)
            own_piece(block).wait()
            copies[0]().wait_recv()
            copies[2]().start()
            copies[1]().wait_recv()
            copies[3]().start()

    def stage_spread_core(block):
        @pl.when(me == HOLDER[block])
        def _():
            copies = gather(block)
            copies[2]().wait_recv()
            copies[3]().wait_recv()
            copies[4]().start()

    def finish(block):
        for copy in scatter(block):
            copy().wait_send()

        @pl.when(me != HOLDER[block])
        def _():
            to_line(block, 1).wait_send()

        @pl.when(me == HOLDER[block])
        def _():
            copies = gather(block)
            copies[4]().wait_recv()
            for copy in copies:
                copy().wait_send()

    stages = (
        [stage_core, stage_one, stage_two, stage_three]
        + [partial(stage_line, hop) for hop in range(sections)]
        + [stage_spread, stage_spread_two, stage_spread_core]
    )
    for tick in range(len(order) + len(stages) - 1):
        for place, stage in enumerate(stages):
            if 0 <= tick - place < len(order):
                stage(order[tick - place])
        if tick == 2:

            @pl.loop(1, replicas)
            def _(step):
                pack_copy(step).start()

        if tick == 4:
            own_small.wait()

            @pl.loop(1, replicas)
            def _(step):
                small_copy(step).wait()

            small_sum[...] = jnp.sum(small_all[...], axis=0)
            for step in range(1, sections):
                remote(
                    small_sum, smalls.at[me], sum_send.at[step], sum_recv.at[step],
                    others[step - 1],
                ).start()
            pltpu.make_async_copy(small_sum, smalls.at[me], sum_send.at[0]).start()
    for block in order:
        finish(block)
    for step in range(1, sections):
        remote(
            small_sum, smalls.at[me], sum_send.at[step], sum_recv.at[step], others[step - 1]
        ).wait()
    pltpu.make_async_copy(small_sum, smalls.at[me], sum_send.at[0]).wait()
    own_pack.wait()

    @pl.loop(1, replicas)
    def _(step):
        pack_copy(step).wait()


def reduce_grads(sections, replicas, parts, pack, small):
    order = (8, 10, 9, 11, 4, 5, 6, 7, 0, 1, 2, 3)
    groups = replicas // CUBE
    owned = len(OWN[0])
    cube = (2, 2, 2, PIECE, D)
    low = jnp.bfloat16
    dma = pltpu.SemaphoreType.DMA
    return pl.pallas_call(
        partial(reduce_kernel, sections, replicas, order),
        out_shape=(
            jax.ShapeDtypeStruct((owned,) + cube, low),
            jax.ShapeDtypeStruct((replicas,) + pack.shape, low),
            jax.ShapeDtypeStruct((sections,) + small.shape, jnp.float32),
        ),
        in_specs=[pl.BlockSpec(memory_space=pl.ANY)] * 3,
        out_specs=[pl.BlockSpec(memory_space=pl.ANY)] * 3,
        scratch_shapes=[
            pltpu.VMEM((REDUCED, 2, 2, PIECE, D), low),
            pltpu.VMEM((REDUCED, 2, 2, PIECE, D), low),
            pltpu.VMEM((REDUCED, 2, HALF, D), low),
            pltpu.VMEM((REDUCED, 2, HALF, D), low),
            pltpu.VMEM((REDUCED, HALF, D), low),
            pltpu.VMEM((REDUCED, HALF, D), low),
            pltpu.VMEM((REDUCED, 2, PIECE, D), low),
            pltpu.VMEM((REDUCED, max(groups - 1, 1), PIECE, D), low),
            pltpu.VMEM((replicas,) + small.shape, jnp.float32),
            pltpu.VMEM(small.shape, jnp.float32),
            dma((REDUCED,)),
            dma((REDUCED, 5)),
            dma((REDUCED, 5)),
            dma((REDUCED,)),
            dma((REDUCED, 2)),
            dma((REDUCED, max(groups - 1, 1))),
            dma((REDUCED, max(groups - 1, 1))),
            dma((owned, 5)),
            dma((owned, 5)),
            dma((owned,)),
            dma((replicas,)),
            dma((replicas,)),
            dma((replicas,)),
            dma((replicas,)),
            dma((sections,)),
            dma((sections,)),
        ],
        compiler_params=pltpu.CompilerParams(
            collective_id=1, has_side_effects=True, vmem_limit_bytes=56 * 1024 * 1024
        ),
    )(parts.reshape((REDUCED,) + cube), pack, small)


def passed_along(value, axis, steps):
    count = lax.axis_size(axis)
    leading, last = (max(0, -steps), min(count, count - steps))
    return lax.ppermute(value, axis, [(source, source + steps) for source in range(leading, last)])


def normalize(summed, gain_row, bias_row):
    average = jnp.mean(summed, axis=-1, keepdims=True)
    centred = summed - average
    inv_dev = lax.rsqrt(jnp.mean(centred * centred, axis=-1, keepdims=True) + 1e-05)
    normed = centred * inv_dev
    return (normed * gain_row + bias_row, normed, inv_dev)


def normalize_backward(grad_out, normed, inv_dev, gain_row):
    grad_full = grad_out.astype(jnp.float32)
    grad_gain = jnp.sum(grad_full * normed, axis=0)
    grad_bias = jnp.sum(grad_full, axis=0)
    grad_normed = grad_full * gain_row
    grad_sum = inv_dev * (
        grad_normed
        - jnp.mean(grad_normed, axis=-1, keepdims=True)
        - normed * jnp.mean(grad_normed * normed, axis=-1, keepdims=True)
    )
    return (grad_sum, grad_gain, grad_bias)


def attention_forward(hidden, w_qkv, w_out, gain_row, bias_row, allowed, groups):
    row_count = hidden.shape[0]
    length = row_count // groups
    head_dim = D // HEADS
    qkv_all = jnp.dot(hidden, w_qkv, preferred_element_type=jnp.float32).astype(jnp.bfloat16)
    split = qkv_all.reshape(groups, length, 3, HEADS, head_dim)
    queries = split[:, :, 0]
    keys_all = split[:, :, 1]
    values = split[:, :, 2]
    scores = jnp.einsum(
        "glhd,gmhd->ghlm", queries, keys_all, preferred_element_type=jnp.float32
    ) * head_dim ** (-0.5)
    if allowed is not None:
        scores = jnp.where(allowed, scores, -1000000000.0)
    attn_probs = jax.nn.softmax(scores, axis=-1)
    probs_low = attn_probs.astype(jnp.bfloat16)
    context = jnp.einsum("ghlm,gmhd->glhd", probs_low, values, preferred_element_type=jnp.float32)
    context = context.reshape(row_count, D).astype(jnp.bfloat16)
    branch = lax.dot_general(
        context, w_out, (((1,), (1,)), ((), ())), preferred_element_type=jnp.float32
    )
    output, normed, inv_dev = normalize(hidden.astype(jnp.float32) + branch, gain_row, bias_row)
    return (output, (queries, keys_all, values, attn_probs, probs_low, context, normed, inv_dev))


def attention_backward(hidden, w_qkv, w_out, gain_row, saved, grad_out, groups):
    queries, keys_all, values, attn_probs, probs_low, context, normed, inv_dev = saved
    row_count = hidden.shape[0]
    length = row_count // groups
    head_dim = D // HEADS
    scale = head_dim ** (-0.5)
    grad_sum, grad_gain, grad_bias = normalize_backward(grad_out, normed, inv_dev, gain_row)
    grad_branch = grad_sum.astype(jnp.bfloat16)
    grad_context = jnp.dot(grad_branch, w_out, preferred_element_type=jnp.float32).astype(
        jnp.bfloat16
    )
    grad_heads = grad_context.reshape(groups, length, HEADS, head_dim)
    grad_probs = jnp.einsum(
        "glhd,gmhd->ghlm", grad_heads, values, preferred_element_type=jnp.float32
    )
    grad_values = jnp.einsum(
        "ghlm,glhd->gmhd", probs_low, grad_heads, preferred_element_type=jnp.float32
    )
    grad_scores = attn_probs * (
        grad_probs - jnp.sum(attn_probs * grad_probs, axis=-1, keepdims=True)
    )
    grad_scores = grad_scores.astype(jnp.bfloat16)
    grad_queries = (
        jnp.einsum("ghlm,gmhd->glhd", grad_scores, keys_all, preferred_element_type=jnp.float32)
        * scale
    )
    grad_keys = (
        jnp.einsum("ghlm,glhd->gmhd", grad_scores, queries, preferred_element_type=jnp.float32)
        * scale
    )
    grad_qkv = (
        jnp.stack([grad_queries, grad_keys, grad_values], axis=2)
        .reshape(row_count, 3 * D)
        .astype(jnp.bfloat16)
    )
    grad_hidden = (
        lax.dot_general(
            grad_qkv, w_qkv, (((1,), (1,)), ((), ())), preferred_element_type=jnp.float32
        )
        + grad_sum
    )
    return (grad_hidden, grad_branch, grad_qkv, grad_gain, grad_bias)


def mlp_forward(hidden, w_first, w_second, gain_row, bias_row):
    inner = jnp.dot(hidden, w_first, preferred_element_type=jnp.float32)
    activated = jax.nn.gelu(inner, approximate=False).astype(jnp.bfloat16)
    branch = jnp.dot(activated, w_second, preferred_element_type=jnp.float32)
    output, normed, inv_dev = normalize(hidden.astype(jnp.float32) + branch, gain_row, bias_row)
    return (output, (inner, activated, normed, inv_dev))


def mlp_backward(hidden, w_first, w_second, gain_row, saved, grad_out):
    inner, activated, normed, inv_dev = saved
    grad_sum, grad_gain, grad_bias = normalize_backward(grad_out, normed, inv_dev, gain_row)
    grad_branch = grad_sum.astype(jnp.bfloat16)
    grad_act = lax.dot_general(
        grad_branch, w_second, (((1,), (1,)), ((), ())), preferred_element_type=jnp.float32
    )
    unused_out, gelu_pull = jax.vjp(partial(jax.nn.gelu, approximate=False), inner)
    grad_inner = gelu_pull(grad_act)[0].astype(jnp.bfloat16)
    grad_hidden = (
        lax.dot_general(
            grad_inner, w_first, (((1,), (1,)), ((), ())), preferred_element_type=jnp.float32
        )
        + grad_sum
    )
    return (grad_hidden, grad_branch, grad_inner, grad_gain, grad_bias)


def outer(left, right):
    return lax.dot_general(
        left, right, (((0,), (0,)), ((), ())), preferred_element_type=jnp.float32
    )


def on_device(tokens, cotangent, seg_doc, wide_in, half_out, norm_gain, norm_bias):
    sections = lax.axis_size("section")
    replicas = lax.axis_size("dp")
    me = lax.axis_index("section")
    seg_count = seg_doc.shape[1]
    low = jnp.bfloat16
    own_wide, own_half = wide_in[0], half_out[0]
    own_gain, own_bias = norm_gain[0], norm_bias[0]
    vector = jnp.concatenate([norm_gain, norm_bias, jnp.zeros((6, D), jnp.float32)], axis=0)
    blocks, vectors = gather_weights(sections, own_wide, own_half, vector)

    def wide_of(first):
        return jnp.concatenate([blocks[first + i] for i in range(4)], axis=1)

    w_qkv = jnp.concatenate([blocks[i] for i in range(3)], axis=1)
    w_out = blocks[3]
    w_first = wide_of(4)
    w_second = blocks[8:12].reshape(4 * D, D)
    last_second = jnp.concatenate([blocks[12:14].reshape(2 * D, D), own_half], axis=0)

    first, saved_first = attention_forward(
        tokens, w_qkv, w_out, vectors[0, 0], vectors[0, 1], None, seg_count
    )
    h1 = first.astype(low)
    second, saved_second = mlp_forward(h1, w_first, w_second, vectors[1, 0], vectors[1, 1])
    h2 = second.astype(low)

    def leaders_of(rows):
        return rows.reshape(seg_count, -1, D)[:, 0]

    both = jnp.stack([leaders_of(h2), leaders_of(cotangent)])
    both = lax.all_gather(both, "section", axis=1, tiled=True)
    leaders, lead_cot = both[0], both[1]
    allowed = (seg_doc[:, :, None] == seg_doc[:, None, :])[:, None]
    third, saved_third = attention_forward(
        leaders, own_wide[:, : 3 * D], own_wide[:, 3 * D :], own_gain, own_bias, allowed,
        seg_doc.shape[0],
    )
    h3 = passed_along(third.astype(low), "section", 1)
    fourth, saved_fourth = mlp_forward(h3, own_wide, last_second, own_gain, own_bias)
    grad_h3, lead_branch, lead_inner, gain_fourth, bias_fourth = mlp_backward(
        h3, own_wide, last_second, own_gain, saved_fourth, lead_cot
    )
    grad_third = passed_along(grad_h3.astype(low), "section", -1)
    grad_lead, lead_out_branch, lead_qkv, gain_third, bias_third = attention_backward(
        leaders, own_wide[:, : 3 * D], own_wide[:, 3 * D :], own_gain, saved_third, grad_third,
        seg_doc.shape[0],
    )
    pair = jnp.where(me == sections - 1, fourth, grad_lead).astype(low)
    pairs = lax.all_gather(pair, "section", axis=0)
    mine = lax.dynamic_slice_in_dim(pairs, me * seg_count, seg_count, axis=1)
    lead_out, lead_grad = mine[sections - 1], mine[sections - 2]

    def with_leaders(rows, lead_rows):
        return rows.reshape(seg_count, -1, D).at[:, 0].set(lead_rows).reshape(rows.shape)

    layer_out = with_leaders(h2, lead_out)
    grad_h2 = with_leaders(cotangent, lead_grad)
    grad_h1, gb_second, grad_inner, gain_second, bias_second = mlp_backward(
        h1, w_first, w_second, vectors[1, 0], saved_second, grad_h2
    )
    grad_tokens, gb_first, grad_qkv, gain_first, bias_first = attention_backward(
        tokens, w_qkv, w_out, vectors[0, 0], saved_first, grad_h1.astype(low), seg_count
    )
    context, activated = saved_first[5], saved_second[1]
    grad_blocks = (
        [outer(tokens, grad_qkv[:, i * D : (i + 1) * D]) for i in range(3)]
        + [outer(gb_first, context)]
        + [outer(h1, grad_inner[:, i * D : (i + 1) * D]) for i in range(4)]
        + [outer(activated[:, i * D : (i + 1) * D], gb_second) for i in range(4)]
    )
    parts = jnp.stack([block.astype(low) for block in grad_blocks])

    is_last = me == sections - 1
    act = saved_fourth[1]
    handed = passed_along(jnp.concatenate([act[:, : 2 * D], lead_branch], axis=1), "section", -1)
    pack = jnp.concatenate(
        [
            jnp.where(is_last, h3, leaders),
            jnp.where(is_last, h3, lead_out_branch),
            jnp.where(is_last, lead_inner, jnp.concatenate([lead_qkv, saved_third[5]], axis=1)),
            jnp.where(is_last, act[:, 2 * D :], handed[:, : 2 * D]),
            jnp.where(is_last, lead_branch, handed[:, 2 * D :]),
        ],
        axis=1,
    )
    pack = jnp.concatenate([pack, jnp.zeros((16 - pack.shape[0], PACK), low)], axis=0)
    small = jnp.stack(
        [
            gain_first,
            bias_first,
            gain_second,
            bias_second,
            jnp.where(is_last, gain_fourth, gain_third),
            jnp.where(is_last, bias_fourth, bias_third),
            jnp.zeros_like(gain_first),
            jnp.zeros_like(gain_first),
        ]
    )
    total, packs, smalls = reduce_grads(sections, replicas, parts, pack, small)
    total = total.reshape(-1, D, D)
    packs = packs.reshape(-1, PACK)
    cross = me >= 2
    lead_wide = jnp.concatenate(
        [
            outer(packs[:, :D], packs[:, 2 * D : 5 * D]),
            outer(packs[:, D : 2 * D], packs[:, 5 * D : 6 * D]),
        ],
        axis=1,
    )
    lead_half = outer(packs[:, 6 * D : 8 * D], packs[:, 8 * D :])
    wide_total = jnp.where(
        cross, lead_wide, jnp.concatenate([total[i] for i in range(4)], axis=1).astype(jnp.float32)
    )
    half_total = jnp.where(cross, lead_half, total[4:].reshape(2 * D, D).astype(jnp.float32))
    small_total = jnp.sum(smalls, axis=0)
    own_small = lax.dynamic_index_in_dim(smalls, me, 0, keepdims=False)

    def vector_total(row):
        near = jnp.where(me == 0, small_total[row], small_total[2 + row])
        return jnp.where(cross, own_small[4 + row], near)

    return (
        layer_out,
        grad_tokens.astype(low),
        wide_total[None],
        half_total[None],
        vector_total(0)[None],
        vector_total(1)[None],
    )


def solution(mesh):
    placed = (
        P(("dp", "section"), None),
        P(("dp", "section"), None),
        P("dp", None),
        P("section", None, None),
        P("section", None, None),
        P("section", None),
        P("section", None),
    )
    return jax.shard_map(
        on_device,
        mesh=mesh,
        in_specs=placed,
        out_specs=(
            P(("dp", "section"), None),
            P(("dp", "section"), None),
            P("section", None, None),
            P("section", None, None),
            P("section", None),
            P("section", None),
        ),
        check_vma=False,
    )
```

time: 1130 us -> 588 us (0.52)
  waiting for transfers between devices: 471 us -> 2.37 us
  Pallas kernels: 0 us -> 358 us
  other arithmetic: 148 us -> 28.2 us
  loops' own time: 117 us -> 0 us
  local copies, waits for them, and re-layouts: 179 us -> 66.4 us
  matrix products: 133 us -> 75 us
  starting transfers between devices: 47.2 us -> 7.08 us
  blocking collectives: 13.7 us -> 38.3 us
  between operations: 15.1 us -> 2.35 us
    pallas_call x0 -> x2, Pallas kernels: none -> 358 us  [the longest x1 224 us: gather_weights(): pl.pallas_call(partial(gather_kernel, sections, order), out_shape=(jax.Sh...]
    ppermute x14 -> x3, waiting for transfers between devices: 213 us -> 2.37 us  [passed_along(): lax.ppermute(value, axis, [(source, source + steps) for source in range(l...]
    psum x1 -> x0, waiting for transfers between devices: 199 us -> none  [on_device(): lax.psum((sum_first, sum_second, sum_gain, sum_bias), 'dp')]
    another operation x14 -> x0, loops' own time: 117 us -> none  [the longest x7 75.6 us: on_device(): lax.switch(chosen, backward_fns, kept_inputs[slot], grad_out, seg_doc[slot])]
    all_gather x2 -> x0, waiting for transfers between devices: 52.4 us -> none  [the longest x1 52.4 us: on_device(): lax.all_gather(tokens, 'section', axis=0, tiled=True)]
    broadcast_in_dim x12 -> x1, local copies, waits for them, and re-layouts: 44.1 us -> 0.01 us  [on_device(): jnp.zeros((6, D), jnp.float32)]
    cond x166 -> x0, local copies, waits for them, and re-layouts: 42.8 us -> none  [the longest x4 38.4 us: on_device(): lax.switch(chosen, backward_fns, kept_inputs[slot], grad_out, seg_doc[slot])]
    all_gather x0 -> x2, blocking collectives: none -> 38.3 us  [the longest x1 25.2 us: on_device(): both = lax.all_gather(both, 'section', axis=1, tiled=True)]
  transfers between devices with their start and end apart: 19 -> 3, of which waited for: 17 -> 1; matrix products, arithmetic and copies ran while one was open for 7% -> 11% of each run, Pallas kernels for 0% -> 0%
where the time goes in v1:
time: 588 us; the launch traced here: 578 us
  Pallas kernels  358 us (61%)
  matrix products  75 us (13%)
  local copies, waits for them, and re-layouts  66.4 us (11%)
  blocking collectives  38.3 us (7%)
  other arithmetic  28.2 us (5%)
  starting transfers between devices  7.08 us (1%)
    pallas_call x1, Pallas kernels, gather_weights(): pl.pallas_call(partial(gather_kernel, sections, order), out_shape=(jax.Sh...  224 us
    pallas_call x1, Pallas kernels, reduce_grads(): pl.pallas_call(partial(reduce_kernel, sections, replicas, order), out_sha...  134 us
    all_gather x1, blocking collectives, on_device(): both = lax.all_gather(both, 'section', axis=1, tiled=True)  25.2 us
    unnamed x202, local copies, waits for them, and re-layouts  19.1 us
    dot_general x15, matrix products, outer(): lax.dot_general(left, right, (((0,), (0,)), ((), ())), preferred_element_...  17 us
    dot_general x2, matrix products, mlp_forward(): inner = jnp.dot(hidden, w_first, preferred_element_type=jnp.float32)  15.6 us
    all_gather x1, blocking collectives, on_device(): pairs = lax.all_gather(pair, 'section', axis=0)  13.1 us
  transfers between devices with their start and end apart: 3, of which 1 were waited for; matrix products, arithmetic and copies ran while one was open for 11% of the time, Pallas kernels for 0%

profile of v1, /device:TPU:0, one launch (start us, length us, event | category | flops | bytes accessed | tf_op | source)
XLA Modules:
  0.0 577.9 jit_solution(9803983346406788900)
XLA Ops:
  5.1 224.0 %shard_map.118 = (bf16[14,2,2,2,96,768]{5,4,3,2,1,0:T(8,128)(2,1)}, f32[4,8,768]{2,1,0:T(8,128)}) custom-call(bf16[768,3072]{1,0:T(8,128)(2,1)} %bitcast.245, bf16[1536,768]{1,0:T(8,128)(2,1)} %bitcast.288, f32[8,768]{1,0:T(8,128)} %maximum_maximum_fusion.vector), custom_call_target="tpu_custom_call" | custom-call | tf_op jit(solution)/shard_map/pallas_call | solution.py:215
  229.1 4.9 slice.254
  234.1 6.7 %fusion.130 = (bf16[1,2,2,2,96,768]{5,4,3,2,1,0:T(8,128)(2,1)}, bf16[1,2,2,2,96,768]{5,4,3,2,1,0:T(8,128)(2,1)}, bf16[1,2,2,2,96,768]{5,4,3,2,1,0:T(8,128)(2,1)}...) fusion(bf16[14,2,2,2,96,768]{5,4,3,2,1,0:T(8,128)(2,1)} %get-tu, ...), kind=kLoop, calls=%fused_computation.277 | loop fusion | bytes 18874368 | tf_op jit(solution)/shard_map/slice | solution.py:682
  243.6 4.1 fusion.3
  247.7 3.5 reshape.403
  251.3 2.2 fusion.132
  259.7 12.3 %multiply_convert_fusion = (bf16[256,3072]{1,0:T(8,128)(2,1)S(1)}, f32[256,3072]{1,0:T(8,128)}, f32[256,3072]{1,0:T(8,128)}) fusion(bf16[256,768]{1,0:T(8,128)(2,1)S(1)} %add_convert_fusion.2, bf16[768,768]{1,0:T(8,128)(2,1)S(1)} %bitcast.302, bf16[768,768]{1,0:T(8,128)(2,1)S(1)} %bitcast.304, bf16[768,768]{1,0:T(8,128)(2,1)S(1)} %bitcast.306, ...), kind=kOutput, calls=%fused_computation.15 | convolution fusion | flops 1277952000 | bytes 12976128 | tf_op jit(solution)/shard_map/dot_general | solution.py:639
  274.9 25.2 %all_gather.9 = bf16[2,8,768]{2,0,1:T(2,128)(2,1)S(1)} all-gather(bf16[2,2,768]{2,0,1:T(2,128)(2,1)S(1)} %copy.152), channel_id=1, replica_groups=mesh['dp'=8,'section'=4] {'section'}, dimensions={1}, use_global_device_ids=true | all-gather | bytes 30720 | tf_op jit(solution)/shard_map/all_gather | solution.py:701
  305.5 2.3 fusion.138
  315.0 4.5 collective-permute-start
  320.8 3.3 slice.265
  324.1 3.3 multiply_convert_fusion.2
  337.6 2.4 collective-permute-done.1
  351.4 3.1 fusion.44
  354.5 13.1 %all-gather = bf16[32,768]{1,0:T(8,128)(2,1)S(1)} all-gather(bf16[8,768]{1,0:T(8,128)(2,1)S(1)} %fusion.44), channel_id=2, replica_groups=mesh['dp'=8,'section'=4] {'section'}, dimensions={0}, use_global_device_ids=true | all-gather | bytes 61440 | tf_op jit(solution)/shard_map/all_gather | solution.py:719
  374.5 5.4 add_convert_fusion
  380.0 2.2 multiply_reduce_fusion.1
  385.0 2.2 fusion.27
  417.5 134.2 %shard_map.119 = (bf16[6,2,2,2,96,768]{5,4,3,2,1,0:T(8,128)(2,1)}, bf16[8,16,6912]{2,1,0:T(8,128)(2,1)}, f32[4,8,768]{2,1,0:T(8,128)}) custom-call(bf16[12,2,2,2,96,768]{5,4,3,2,1,0:T(8,128)(2,1)} %constant_dynamic-update-slice_fusion.parts, bf16[16,6912]{1,0:T(8,128)(2,1)} %concatenate.68.pack, f32[8,768]{1,0:T(8,128)} %stack.121.small), custom_call_target="tpu_custom_call" | custom-call | tf_op jit(solution)/shard_map/pallas_call | solution.py:499
  551.7 3.2 slice.294
  555.0 4.4 fusion.131
  559.8 4.1 convolution_bitcast_fusion
  565.4 5.0 fusion.2
  571.8 5.9 %maximum_select_fusion = f32[1,768,3072]{2,1,0:T(8,128)} fusion(f32[1,768,768]{2,1,0:T(8,128)S(1)} %convolution_bitcast_fusion.1, f32[1,768,2304]{2,1,0:T(8,128)S(1)} %copy-done, bf16[1,768,768]{2,1,0:T(8,128)(2,1)} %bitcast.260, bf16[1,768,768]{2,1,0:T(8,128)(2,1)} %bitcast.261, bf16[1,768,768]{2,1,0:T(8,128)(2,1)} %bitcast.262, ...), kind=kLoop, calls=%fused_computation.2 | loop fusion | flops 23592960 | bytes 23592960 | tf_op jit(solution)/shard_map/jit(_where)/select_n | solution.py:781
  (328 shorter events, 94.1 us)
Async XLA Ops:
  234.1 6.8 %copy-start.86 = (s32[4,2]{0,1:T(2,128)S(1)}, s32[4,2]{0,1:T(2,128)}, u32[]{:S(2)}) copy-start(s32[4,2]{0,1:T(2,128)} %param.13) | copy-start | bytes 100
  234.1 9.6 %copy-start.2 = (bf16[256,768]{1,0:T(8,128)(2,1)S(1)}, bf16[256,768]{1,0:T(8,128)(2,1)}, u32[]{:S(2)}) copy-start(bf16[256,768]{1,0:T(8,128)(2,1)} %param.11) | copy-start | bytes 1179652
  243.6 15.0 %copy-start.52 = (f32[768]{0:T(1024)}, f32[768]{0:T(1024)S(1)}, u32[]{:S(2)}) copy-start(f32[768]{0:T(1024)S(1)} %get-tuple-element.51) | copy-start | bytes 9220
  243.6 30.2 %copy-start.49 = (f32[768]{0:T(1024)}, f32[768]{0:T(1024)S(1)}, u32[]{:S(2)}) copy-start(f32[768]{0:T(1024)S(1)} %get-tuple-element.48) | copy-start | bytes 9220
  257.7 14.3 %copy-start.5 = (bf16[2,128,12,64]{1,0,3,2:T(2,128)(2,1)}, bf16[2,128,12,64]{1,0,3,2:T(2,128)(2,1)S(1)}, u32[]{:S(2)}) copy-start(bf16[2,128,12,64]{1,0,3,2:T(2,128)(2,1)S(1)} %copy.150) | copy-start | bytes 1179652
  258.3 13.7 %copy-start.59 = (f32[256]{0:T(256)}, f32[256]{0:T(256)S(1)}, u32[]{:S(2)}) copy-start(f32[256]{0:T(256)S(1)} %broadcast_multiply_fusion.4) | copy-start | bytes 3076
  258.3 13.7 %slice-start.4 = ((s8[4718592]{0:T(1024)(128)(4,1)}), s8[4194304]{0:T(1024)(128)(4,1)S(1)}, s32[]{:S(2)}) async-start(s8[4718592]{0:T(1024)(128)(4,1)} %bitcast.264), calls=%async_computation.4 | async-start | bytes 8388608
  258.4 43.0 %slice-start = ((s8[4718592]{0:T(1024)(128)(4,1)}), s8[4194304]{0:T(1024)(128)(4,1)S(1)}, s32[]{:S(2)}) async-start(s8[4718592]{0:T(1024)(128)(4,1)} %bitcast.248), calls=%async_computation | async-start | bytes 8388608
  258.6 13.4 %copy-start.74 = (f32[256]{0:T(256)}, f32[256]{0:T(256)S(1)}, u32[]{:S(2)}) copy-start(f32[256]{0:T(256)S(1)} %add_rsqrt_fusion.1) | copy-start | bytes 3076
  259.7 12.3 %slice-start.5 = ((s8[4718592]{0:T(1024)(128)(4,1)}), s8[524288]{0:T(1024)(128)(4,1)S(1)}, s32[]{:S(2)}) async-start(s8[4718592]{0:T(1024)(128)(4,1)} %bitcast.264), calls=%async_computation.5 | async-start | bytes 1048576
  259.7 41.6 %slice-start.1 = ((s8[4718592]{0:T(1024)(128)(4,1)}), s8[524288]{0:T(1024)(128)(4,1)S(1)}, s32[]{:S(2)}) async-start(s8[4718592]{0:T(1024)(128)(4,1)} %bitcast.248), calls=%async_computation.1 | async-start | bytes 1048576
  273.6 27.1 %copy-start.54 = (f32[256]{0:T(256)}, f32[256]{0:T(256)S(1)}, u32[]{:S(2)}) copy-start(f32[256]{0:T(256)S(1)} %broadcast_multiply_fusion.3) | copy-start | bytes 3076
  273.8 35.8 %copy-start.68 = (f32[256]{0:T(256)}, f32[256]{0:T(256)S(1)}, u32[]{:S(2)}) copy-start(f32[256]{0:T(256)S(1)} %add_rsqrt_fusion) | copy-start | bytes 3076
  311.2 8.3 %copy-start.45 = (bf16[8,768]{1,0:T(8,128)(2,1)}, bf16[8,768]{1,0:T(8,128)(2,1)S(1)}, u32[]{:S(2)}) copy-start(bf16[8,768]{1,0:T(8,128)(2,1)S(1)} %convert_element_type.211) | copy-start | bytes 36868
  313.0 6.5 %copy-start.69 = (f32[8]{0:T(128)}, f32[8]{0:T(128)S(1)}, u32[]{:S(2)}) copy-start(f32[8]{0:T(128)S(1)} %broadcast_multiply_fusion.10) | copy-start | bytes 100
  313.6 7.2 %copy-start.76 = (f32[8]{0:T(128)}, f32[8]{0:T(128)S(1)}, u32[]{:S(2)}) copy-start(f32[8]{0:T(128)S(1)} %add_rsqrt_fusion.3) | copy-start | bytes 100
  315.0 9.1 %collective-permute-start = (bf16[8,768]{1,0:T(8,128)(2,1)}, bf16[8,768]{1,0:T(8,128)(2,1)}, u32[]{:S(2)}, u32[]{:S(2)}) collective-permute-start(bf16[8,768]{1,0:T(8,128)(2,1)} %add_convert_fusion.4), channel_id=1, source_target_pairs={{0,1},{1,2},{2,3},{4,5},{5,6},{6,7},{8,9},{9,10},{10,11},{12,13},{... | collective-permute-start | bytes 36872 | tf_op jit(solution)/shard_map/ppermute | solution.py:545
  332.4 7.6 %copy-start.31 = (f32[8,768]{1,0:T(8,128)S(1)}, f32[8,768]{1,0:T(8,128)}, u32[]{:S(2)}) copy-start(f32[8,768]{1,0:T(8,128)} %copy-done.30) | copy-start | bytes 73732
  332.4 7.6 %copy-start.70 = (f32[8]{0:T(128)S(1)}, f32[8]{0:T(128)}, u32[]{:S(2)}) copy-start(f32[8]{0:T(128)} %copy-done.69) | copy-start | bytes 100
  332.4 7.6 %copy-start.77 = (f32[8]{0:T(128)S(1)}, f32[8]{0:T(128)}, u32[]{:S(2)}) copy-start(f32[8]{0:T(128)} %copy-done.76) | copy-start | bytes 100
  334.4 5.6 collective-permute-start.1
  335.7 79.7 %collective-permute-start.2 = (bf16[8,2304]{1,0:T(8,128)(2,1)}, bf16[8,2304]{1,0:T(8,128)(2,1)}, u32[]{:S(2)}, u32[]{:S(2)}) collective-permute-start(bf16[8,2304]{1,0:T(8,128)(2,1)} %pad_maximum_fusion.17), channel_id=1, source_target_pairs={{1,0},{2,1},{3,2},{5,4},{6,5},{7,6},{9,8},{10,9},{11,10},{13,12},{... | collective-permute-start | bytes 110600 | tf_op jit(solution)/shard_map/ppermute | solution.py:545
  409.9 6.2 %copy-start.48 = (bf16[8,768]{1,0:T(8,128)(2,1)S(1)}, bf16[8,768]{1,0:T(8,128)(2,1)}, u32[]{:S(2)}) copy-start(bf16[8,768]{1,0:T(8,128)(2,1)} %copy-done.47) | copy-start | bytes 36868
  565.4 6.4 %copy-start = (f32[1,768,2304]{2,1,0:T(8,128)S(1)}, f32[1,768,2304]{2,1,0:T(8,128)}, u32[]{:S(2)}) copy-start(f32[1,768,2304]{2,1,0:T(8,128)} %convolution_bitcast_fusion) | copy-start | bytes 21233668
  (73 other events, 198.2 us)

commit v2 on v0

v2 whole, which is shorter than its diff:
```python
from functools import partial

import jax
import jax.numpy as jnp
from jax import lax
from jax.experimental import pallas as pl
from jax.experimental.pallas import tpu as pltpu
from jax.sharding import PartitionSpec as P

D = 768
HEADS = 12
PAIRS = HEADS // 2
CUBE = 8
PIECE = D // CUBE
HALF = PIECE // 2
SLAB = 16
HOLDER = (0, 0, 0, 0, 1, 1, 1, 1, 0, 0, 1, 1, 2, 2)
GATHERED = len(HOLDER)
REDUCED = 12
OWN = {0: (0, 1, 2, 3, 8, 9), 1: (4, 5, 6, 7, 10, 11)}
OWNED = len(OWN[0])
LEFT_OUT, RIGHT, LEFT_HALF, RIGHT_HALF, PACK = D, 2 * D, 6 * D, 8 * D, 9 * D
LOW = jnp.bfloat16
F32 = jnp.float32
DMA = pltpu.SemaphoreType.DMA
MESH = pl.DeviceIdType.MESH


def dot(left, right):
    return jnp.dot(left, right, preferred_element_type=F32)


def dot_right(left, right):
    return lax.dot_general(left, right, (((1,), (1,)), ((), ())), preferred_element_type=F32)


def outer(left, right):
    return lax.dot_general(left, right, (((0,), (0,)), ((), ())), preferred_element_type=F32)


def normalize(summed, gain, bias):
    average = jnp.mean(summed, axis=-1, keepdims=True)
    centred = summed - average
    inv_dev = lax.rsqrt(jnp.mean(centred * centred, axis=-1, keepdims=True) + 1e-05)
    normed = centred * inv_dev
    return normed * gain + bias, normed, inv_dev


def normalize_backward(grad, normed, inv_dev, gain):
    scaled = grad * gain
    mean_scaled = jnp.mean(scaled, axis=-1, keepdims=True)
    mean_normed = jnp.mean(scaled * normed, axis=-1, keepdims=True)
    grad_sum = inv_dev * (scaled - mean_scaled - normed * mean_normed)
    return (
        grad_sum,
        jnp.sum(grad * normed, axis=0, keepdims=True),
        jnp.sum(grad, axis=0, keepdims=True),
    )


def gelu_pair(value):
    bell = jnp.exp(-0.5 * value * value)
    base = 1.0 + (0.3275911 * 0.7071067811865476) * jnp.abs(value)
    guess = pl.reciprocal(base, approx=True)
    t = guess * (2.0 - base * guess)
    poly = t * (
        0.5 * 0.254829592
        + t
        * (
            0.5 * -0.284496736
            + t * (0.5 * 1.421413741 + t * (0.5 * -1.453152027 + t * (0.5 * 1.061405429)))
        )
    )
    tail = poly * bell
    below = jnp.where(value >= 0, 1.0 - tail, tail)
    return value * below, below + value * bell * 0.3989422804014327


def position():
    index = lax.axis_index("dp")
    return (lax.rem(index // 4, 2), lax.rem(index // 2, 2), lax.rem(index, 2), index // CUBE)


def remote(source, target, send, receive, device):
    return pltpu.make_async_remote_copy(
        src_ref=source,
        dst_ref=target,
        send_sem=send,
        recv_sem=receive,
        device_id=device,
        device_id_type=MESH,
    )


def layer_kernel(
    sections, replicas,
    tokens, cotangent, code, vector, wide, half,
    layer_out, grad_tokens, total, packs, smalls, group_in,
    blocks, own, core_in, one_a, one_b, two_a, two_b, line_in, vectors,
    qkv, probs, context, h1, norm0, dev0, summed, act, slope, norm1, dev1, branch, kept,
    cot_slab, h1_slab, h2_slab, cot_leads, h1_leads, h2_leads,
    lead_third, lead_fourth, lead_grad3, lead_grad2, lead_grad1, handed,
    lead_qkv, lead_probs, lead_context, lead_norm, lead_dev, lead_act, lead_slope, pack,
    small, small_all, small_sum, group_piece,
    line_send, line_recv, cube_send, cube_recv, load_sem,
    rs_send, rs_recv, z_send, z_recv, group_send, group_recv, group_load, ag_send, ag_recv,
    out_sem, pack_send, pack_recv, small_send, small_recv, sum_send, sum_recv,
    vector_send, vector_recv, lead_send, lead_recv, spread_send, spread_recv, hop_send, hop_recv,
    credit,
):
    me = lax.axis_index("section")
    index = lax.axis_index("dp")
    y, x, core, group = position()
    groups = replicas // CUBE
    rows_all = tokens.shape[0]
    seg_rows = rows_all // 2

    def cube_peer(yy, xx, cc):
        return {"dp": group * CUBE + yy * 4 + xx * 2 + cc}

    beside_x = cube_peer(y, 1 - x, core)
    beside_y = cube_peer(1 - y, x, core)
    beside_core = cube_peer(y, x, 1 - core)
    others = [{"section": lax.rem(me + step, sections)} for step in range(1, sections)]

    def replica(step):
        return {"dp": lax.rem(index + step, replicas)}

    barrier = pltpu.get_barrier_semaphore()
    for other in others:
        pl.semaphore_signal(barrier, inc=1, device_id=other, device_id_type=MESH)

    @pl.loop(1, replicas)
    def _(step):
        pl.semaphore_signal(barrier, inc=1, device_id=replica(step), device_id_type=MESH)

    def held(block):
        if block < 8:
            return wide.at[:, :, :, :, pl.ds((block % 4) * D, D)]
        return half.at[block % 2]

    def load(block):
        return pltpu.make_async_copy(held(block), blocks.at[block], load_sem.at[block])

    def load_own(place):
        return pltpu.make_async_copy(
            held(place if place < 4 else 4 + place), own.at[place], load_sem.at[place]
        )

    for holder in (0, 1):

        @pl.when(me == holder)
        def _():
            for block in OWN[holder]:
                load(block).start()

    @pl.when(me >= 2)
    def _():
        for place in range(4):
            load_own(place).start()

    @pl.when(me == 3)
    def _():
        for place in (4, 5):
            load_own(place).start()

    pl.semaphore_wait(barrier, sections - 1 + replicas - 1)

    row_of = lax.broadcasted_iota(jnp.int32, (SLAB, D), 0)

    def lead_rows(ref):
        first = ref[0:SLAB].astype(F32)[0:1]
        second = ref[seg_rows : seg_rows + SLAB].astype(F32)[0:1]
        return jnp.where(row_of == 0, first, jnp.where(row_of == 1, second, 0.0)).astype(LOW)

    def lead_copy(kind, slab, target, reader):
        return remote(
            slab, target.at[me], lead_send.at[kind], lead_recv.at[kind, me], {"section": reader}
        )

    def lead_start(kind, slab, target, reader):
        @pl.when(me != reader)
        def _():
            lead_copy(kind, slab, target, reader).start()

        @pl.when(me == reader)
        def _():
            target[reader] = slab[...]

    def lead_wait(kind, slab, target, reader):
        for section in range(sections):
            if section != reader:
                remote(
                    slab, target.at[section], lead_send.at[kind], lead_recv.at[kind, section],
                    {"section": section},
                ).wait_recv()

    def collected(target):
        value = jnp.zeros((SLAB, D), F32)
        for section in range(sections):
            slab = target[section].astype(F32)
            for lead in range(2):
                value = jnp.where(row_of == 2 * section + lead, slab[lead : lead + 1], value)
        return value

    def spread_copy(kind, slab, step):
        return remote(
            slab, slab, spread_send.at[kind, step], spread_recv.at[kind], others[step - 1]
        )

    def hop_copy(kind, slab, step):
        return remote(
            slab, slab, hop_send.at[kind], hop_recv.at[kind],
            {"section": lax.rem(me + step + sections, sections)},
        )

    def my_leads(slab):
        value = slab[...].astype(F32)
        return [
            jnp.sum(jnp.where(row_of == 2 * me + lead, value, 0.0), axis=0, keepdims=True)
            for lead in range(2)
        ]

    COT, H1, H2 = 0, 1, 2
    FOURTH, GRAD1 = 0, 1
    THIRD, GRAD3, GRAD2, HAND = 0, 1, 2, 3

    def vector_copy(step):
        return remote(
            vector, vectors.at[me], vector_send.at[step], vector_recv.at[step], others[step - 1]
        )

    for step in range(1, sections):
        vector_copy(step).start()
    vectors[me] = vector[...]
    cot_slab[...] = lead_rows(cotangent)
    lead_start(COT, cot_slab, cot_leads, 3)

    upper, lower = pl.ds(0, HALF), pl.ds(HALF, HALF)

    def place_of(block):
        return blocks.at[block] if block < REDUCED else own.at[block - REDUCED + 6]

    def line_copy(block, step, from_holder):
        piece = place_of(block).at[y, x, core]
        if not from_holder:
            source = piece
        elif block < 8:
            source = wide.at[y, x, core, :, pl.ds((block % 4) * D, D)]
        else:
            source = half.at[block % 2, y, x, core]
        return remote(
            source,
            piece,
            line_send.at[block, 0 if step > 0 else 1],
            line_recv.at[block],
            {"section": lax.rem(me + step + sections, sections)},
        )

    def cube_copy(block, stage):
        full = place_of(block)
        ref, peer = (
            (full.at[y, x, core, upper], beside_x),
            (full.at[y, x, core, lower], beside_y),
            (full.at[y, :, core, upper], beside_y),
            (full.at[:, x, core, lower], beside_x),
            (full.at[:, :, core], beside_core),
        )[stage]
        return remote(ref, ref, cube_send.at[block, stage], cube_recv.at[block, stage], peer)

    def gets(block):
        return me > HOLDER[block] if block >= REDUCED else me != HOLDER[block]

    def gather_line(block):
        holder = HOLDER[block]

        @pl.when(me == holder)
        def _():
            line_copy(block, 1, True).start()
            if holder > 0 and block < REDUCED:
                line_copy(block, -1, True).start()

        @pl.when(me > holder)
        def _():
            copy = line_copy(block, 1, False)
            copy.wait_recv()

            @pl.when(me < sections - 1)
            def _():
                copy.start()

        if holder > 0 and block < REDUCED:

            @pl.when(me < holder)
            def _():
                copy = line_copy(block, -1, False)
                copy.wait_recv()

                @pl.when(me > 0)
                def _():
                    copy.start()

    def gather_one(block):
        @pl.when(gets(block))
        def _():
            cube_copy(block, 0).start()
            cube_copy(block, 1).start()

    def gather_two(block):
        @pl.when(gets(block))
        def _():
            cube_copy(block, 0).wait_recv()
            cube_copy(block, 2).start()
            cube_copy(block, 1).wait_recv()
            cube_copy(block, 3).start()

    def gather_three(block):
        @pl.when(gets(block))
        def _():
            cube_copy(block, 2).wait_recv()
            cube_copy(block, 3).wait_recv()
            cube_copy(block, 4).start()

    def gather_ready(block):
        @pl.when(gets(block))
        def _():
            cube_copy(block, 4).wait_recv()

        if block < REDUCED:

            @pl.when(me == HOLDER[block])
            def _():
                load(block).wait()

    def gather_finish(block):
        holder = HOLDER[block]

        @pl.when(gets(block))
        def _():
            for stage in range(5):
                cube_copy(block, stage).wait_send()

        @pl.when(me == holder)
        def _():
            line_copy(block, 1, True).wait_send()
            if holder > 0 and block < REDUCED:
                line_copy(block, -1, True).wait_send()

        @pl.when((me > holder) & (me < sections - 1))
        def _():
            line_copy(block, 1, False).wait_send()

    gather_order = tuple(range(GATHERED))
    gather_stages = (gather_line, gather_one, gather_two, gather_three)

    def gather_tick(tick):
        for place, stage in enumerate(gather_stages):
            if 0 <= tick - place < GATHERED:
                stage(gather_order[tick - place])
        if 0 <= tick - 4 < GATHERED:
            gather_ready(gather_order[tick - 4])

    def weight(block):
        return blocks[block].reshape(D, D)

    lane_of = lax.broadcasted_iota(jnp.int32, (1, 128), 1)
    first_half = lane_of < 64
    head_masks = (first_half.astype(LOW), (~first_half).astype(LOW))

    def chunks(count, body):
        size = rows_all // count

        @pl.loop(0, count)
        def _(step):
            body(pl.multiple_of(step * size, size), size)

    def project(block):
        qkv[:, block * D : (block + 1) * D] = dot(tokens[...], weight(block)).astype(LOW)

    def pair_slices(seg, pair):
        rows = pl.ds(seg * seg_rows, seg_rows)
        return rows, [
            pl.ds(pl.multiple_of(part * D + pair * 128, 128), 128) for part in range(3)
        ]

    def heads_forward(seg):
        @pl.loop(0, PAIRS)
        def _(pair):
            rows, (at_q, at_k, at_v) = pair_slices(seg, pair)
            query, key, value = qkv[rows, at_q], qkv[rows, at_k], qkv[rows, at_v]
            parts = []
            for place in range(2):
                scores = dot_right(query * head_masks[place], key) * 0.125
                raised = jnp.exp(scores - jnp.max(scores, axis=-1, keepdims=True))
                prob = raised / jnp.sum(raised, axis=-1, keepdims=True)
                probs[seg, pair, place] = prob
                parts.append(dot(prob.astype(LOW), value))
            context[rows, at_q] = jnp.where(first_half, parts[0], parts[1]).astype(LOW)

    def attention_close():
        summed[...] = dot_right(context[...], weight(3))
        gain, bias = vectors[0, 0:1], vectors[0, 1:2]

        def body(start, size):
            rows = pl.ds(start, size)
            out, normed, inv_dev = normalize(
                tokens[rows].astype(F32) + summed[rows], gain, bias
            )
            norm0[rows] = normed
            dev0[rows] = jnp.broadcast_to(inv_dev, (size, 128))
            h1[rows] = out.astype(LOW)

        chunks(8, body)

    def inner_block(block):
        summed[...] = dot(h1[...], weight(4 + block))
        lanes = slice(block * D, (block + 1) * D)

        def body(start, size):
            rows = pl.ds(start, size)
            value, grade = gelu_pair(summed[rows])
            act[rows, lanes] = value.astype(LOW)
            slope[rows, lanes] = grade

        chunks(8, body)

    def second_block(block):
        product = dot(act[:, block * D : (block + 1) * D], weight(8 + block))
        if block == 0:
            branch[...] = product
        else:
            branch[...] += product

    def mlp_close():
        gain, bias = vectors[1, 0:1], vectors[1, 1:2]

        def body(start, size):
            rows = pl.ds(start, size)
            out, normed, inv_dev = normalize(h1[rows].astype(F32) + branch[rows], gain, bias)
            norm1[rows] = normed
            dev1[rows] = jnp.broadcast_to(inv_dev, (size, 128))
            layer_out[rows] = out.astype(LOW)

        chunks(8, body)

    def add_small(row, value):
        small[row : row + 1] += value

    def mlp_open_backward():
        gain = vectors[1, 0:1]

        def body(start, size):
            rows = pl.ds(start, size)
            place = start + lax.broadcasted_iota(jnp.int32, (size, D), 0)
            grad = jnp.where(
                lax.rem(place, seg_rows) == 0, 0.0, cotangent[rows].astype(F32)
            )
            grad_sum, grad_gain, grad_bias = normalize_backward(
                grad, norm1[rows], dev1[rows][:, 0:1], gain
            )
            branch[rows] = grad_sum
            kept[rows] = grad_sum.astype(LOW)
            add_small(2, grad_gain)
            add_small(3, grad_bias)

        chunks(8, body)

    def part(block):
        return block + 4 if block < 4 else block + 8

    def store_part(block, value):
        blocks[part(block)] = value.astype(LOW).reshape(2, 2, 2, PIECE, D)

    def second_grad(block):
        store_part(8 + block, outer(act[:, block * D : (block + 1) * D], kept[...]))

    def inner_grad(block):
        lanes = slice(block * D, (block + 1) * D)
        grad_act = dot_right(kept[...], weight(8 + block))
        act[:, lanes] = (grad_act * slope[:, lanes]).astype(LOW)
        branch[...] += dot_right(act[:, lanes], weight(4 + block))
        store_part(4 + block, outer(h1[...], act[:, lanes]))

    def attention_open_backward():
        gain = vectors[0, 0:1]
        leads = my_leads(lead_grad1)

        def body(start, size):
            rows = pl.ds(start, size)
            place = start + lax.broadcasted_iota(jnp.int32, (size, D), 0)
            grad = branch[rows]
            grad = jnp.where(place == 0, leads[0], jnp.where(place == seg_rows, leads[1], grad))
            grad = grad.astype(LOW).astype(F32)
            grad_sum, grad_gain, grad_bias = normalize_backward(
                grad, norm0[rows], dev0[rows][:, 0:1], gain
            )
            summed[rows] = grad_sum
            kept[rows] = grad_sum.astype(LOW)
            add_small(0, grad_gain)
            add_small(1, grad_bias)

        chunks(8, body)

    def out_grad():
        store_part(3, outer(kept[...], context[...]))
        context[...] = dot(kept[...], weight(3)).astype(LOW)

    def heads_backward(seg):
        @pl.loop(0, PAIRS)
        def _(pair):
            rows, (at_q, at_k, at_v) = pair_slices(seg, pair)
            query, key, value = qkv[rows, at_q], qkv[rows, at_k], qkv[rows, at_v]
            grad = context[rows, at_q]
            grads = ([], [], [])
            for place in range(2):
                prob = probs[seg, pair, place]
                grad_prob = dot_right(grad * head_masks[place], value)
                inside = prob * grad_prob
                grad_score = inside - prob * jnp.sum(inside, axis=-1, keepdims=True)
                grad_score = grad_score.astype(LOW)
                grads[0].append(dot(grad_score, key))
                grads[1].append(outer(grad_score, query))
                grads[2].append(outer(prob.astype(LOW), grad))
            for at, pair_grads, scale in zip((at_q, at_k, at_v), grads, (0.125, 0.125, 1.0)):
                merged = jnp.where(first_half, pair_grads[0], pair_grads[1]) * scale
                qkv[rows, at] = merged.astype(LOW)

    def project_grad(block):
        store_part(block, outer(tokens[...], qkv[:, block * D : (block + 1) * D]))

    def tokens_back(block):
        summed[...] += dot_right(qkv[:, block * D : (block + 1) * D], weight(block))

    def leads_mlp_forward(value, first, second, gain, bias):
        total_branch = value.astype(F32)
        for block in range(4):
            lanes = slice(block * D, (block + 1) * D)
            out, grade = gelu_pair(dot(value, first(block)))
            lead_act[:, lanes] = out.astype(LOW)
            lead_slope[:, lanes] = grade
            total_branch = total_branch + dot(lead_act[:, lanes], second(block))
        out, normed, inv_dev = normalize(total_branch, gain, bias)
        lead_norm[...] = normed
        lead_dev[...] = jnp.broadcast_to(inv_dev, (SLAB, 128))
        pack[:, 0:D] = value
        pack[:, LEFT_OUT:RIGHT] = value
        return out

    def leads_mlp_backward(grad, first, second, gain):
        grad_sum, grad_gain, grad_bias = normalize_backward(
            grad, lead_norm[...], lead_dev[:, 0:1], gain
        )
        add_small(4, grad_gain)
        add_small(5, grad_bias)
        low_sum = grad_sum.astype(LOW)
        result = grad_sum
        for block in range(4):
            lanes = slice(block * D, (block + 1) * D)
            grad_inner = (dot_right(low_sum, second(block)) * lead_slope[:, lanes]).astype(LOW)
            pack[:, RIGHT + block * D : RIGHT + (block + 1) * D] = grad_inner
            result = result + dot_right(grad_inner, first(block))
        pack[:, LEFT_HALF:RIGHT_HALF] = lead_act[:, 2 * D :]
        pack[:, RIGHT_HALF:] = low_sum
        handed[:, 0 : 2 * D] = lead_act[:, 0 : 2 * D]
        handed[:, 2 * D :] = low_sum
        return result

    def own_weight(place):
        return own[place].reshape(D, D)

    def last_second(block):
        return own_weight(6 + block if block < 2 else 2 + block)

    def leads_first():
        @pl.when(me == 2)
        def _():
            lead_wait(H2, h2_slab, h2_leads, 2)
            for place in range(4):
                load_own(place).wait()
            value = collected(h2_leads).astype(LOW)
            pack[:, 0:D] = value
            for block in range(3):
                lead_qkv[:, block * D : (block + 1) * D] = dot(value, own_weight(block)).astype(LOW)
            sort = code[...]
            for pair in range(PAIRS):
                at = [slice(p * D + pair * 128, p * D + (pair + 1) * 128) for p in range(3)]
                query, key, val = (lead_qkv[:, lanes] for lanes in at)
                parts = []
                for place in range(2):
                    scores = dot_right(query * head_masks[place], key) * 0.125
                    scores = jnp.where(
                        sort > 1.5, scores, jnp.where(sort > 0.5, -1000000000.0, -1e30)
                    )
                    raised = jnp.exp(scores - jnp.max(scores, axis=-1, keepdims=True))
                    prob = raised / jnp.sum(raised, axis=-1, keepdims=True)
                    lead_probs[pair, place] = prob
                    parts.append(dot(prob.astype(LOW), val))
                lead_context[:, pair * 128 : (pair + 1) * 128] = jnp.where(
                    first_half, parts[0], parts[1]
                ).astype(LOW)
            summed_rows = value.astype(F32) + dot_right(lead_context[...], own_weight(3))
            out, normed, inv_dev = normalize(summed_rows, vectors[2, 0:1], vectors[2, 1:2])
            lead_norm[...] = normed
            lead_dev[...] = jnp.broadcast_to(inv_dev, (SLAB, 128))
            lead_third[...] = out.astype(LOW)
            hop_copy(THIRD, lead_third, 1).start()

        @pl.when(me == 1)
        def _():
            lead_wait(H1, h1_slab, h1_leads, 1)
            leads_mlp_forward(
                collected(h1_leads).astype(LOW),
                lambda block: weight(4 + block),
                lambda block: weight(8 + block),
                vectors[1, 0:1],
                vectors[1, 1:2],
            )

    def leads_second():
        @pl.when(me == 3)
        def _():
            hop_copy(THIRD, lead_third, -1).wait_recv()
            for place in range(6):
                load_own(place).wait()
            out = leads_mlp_forward(
                lead_third[...], own_weight, last_second, vectors[3, 0:1], vectors[3, 1:2]
            )
            lead_fourth[...] = out.astype(LOW)
            for step in range(1, sections):
                spread_copy(FOURTH, lead_fourth, step).start()
            lead_wait(COT, cot_slab, cot_leads, 3)
            grad = leads_mlp_backward(
                collected(cot_leads), own_weight, last_second, vectors[3, 0:1]
            )
            lead_grad3[...] = grad.astype(LOW)
            hop_copy(GRAD3, lead_grad3, -1).start()
            hop_copy(HAND, handed, -1).start()

    def leads_third():
        @pl.when(me == 2)
        def _():
            hop_copy(GRAD3, lead_grad3, 1).wait_recv()
            grad_sum, grad_gain, grad_bias = normalize_backward(
                lead_grad3[...].astype(F32), lead_norm[...], lead_dev[:, 0:1], vectors[2, 0:1]
            )
            add_small(4, grad_gain)
            add_small(5, grad_bias)
            low_sum = grad_sum.astype(LOW)
            pack[:, LEFT_OUT:RIGHT] = low_sum
            pack[:, RIGHT + 3 * D : LEFT_HALF] = lead_context[...]
            grad_context = dot(low_sum, own_weight(3)).astype(LOW)
            for pair in range(PAIRS):
                at = [slice(p * D + pair * 128, p * D + (pair + 1) * 128) for p in range(3)]
                query, key, val = (lead_qkv[:, lanes] for lanes in at)
                grad = grad_context[:, pair * 128 : (pair + 1) * 128]
                grads = ([], [], [])
                for place in range(2):
                    prob = lead_probs[pair, place]
                    grad_prob = dot_right(grad * head_masks[place], val)
                    inside = prob * grad_prob
                    grad_score = inside - prob * jnp.sum(inside, axis=-1, keepdims=True)
                    grad_score = grad_score.astype(LOW)
                    grads[0].append(dot(grad_score, key))
                    grads[1].append(outer(grad_score, query))
                    grads[2].append(outer(prob.astype(LOW), grad))
                for lanes, pair_grads, scale in zip(at, grads, (0.125, 0.125, 1.0)):
                    merged = jnp.where(first_half, pair_grads[0], pair_grads[1]) * scale
                    pack[:, RIGHT + lanes.start : RIGHT + lanes.stop] = merged.astype(LOW)
            result = grad_sum
            for block in range(3):
                result = result + dot_right(
                    pack[:, RIGHT + block * D : RIGHT + (block + 1) * D], own_weight(block)
                )
            lead_grad2[...] = result.astype(LOW)
            hop_copy(GRAD2, lead_grad2, -1).start()
            hop_copy(HAND, handed, 1).wait_recv()
            pack[:, LEFT_HALF:] = handed[...]

    def leads_fourth():
        @pl.when(me == 1)
        def _():
            hop_copy(GRAD2, lead_grad2, 1).wait_recv()
            grad = leads_mlp_backward(
                lead_grad2[...].astype(F32),
                lambda block: weight(4 + block),
                lambda block: weight(8 + block),
                vectors[1, 0:1],
            )
            lead_grad1[...] = grad.astype(LOW)
            for step in range(1, sections):
                spread_copy(GRAD1, lead_grad1, step).start()
            hop_copy(HAND, handed, -1).start()

    def pack_copy(step):
        return remote(
            pack, packs.at[index], pack_send.at[step], pack_recv.at[step], replica(step)
        )

    def own_pack():
        return pltpu.make_async_copy(pack, packs.at[index], pack_send.at[0])

    def leads_close():
        @pl.when(me != 3)
        def _():
            spread_copy(FOURTH, lead_fourth, 1).wait_recv()

        leads = my_leads(lead_fourth)
        for lead in range(2):
            rows = pl.ds(lead * seg_rows, SLAB)
            layer_out[rows] = jnp.where(
                row_of == 0, leads[lead], layer_out[rows].astype(F32)
            ).astype(LOW)

        @pl.when(me != 1)
        def _():
            spread_copy(GRAD1, lead_grad1, 1).wait_recv()

        @pl.when(me == 0)
        def _():
            hop_copy(HAND, handed, 1).wait_recv()
            pack[:, 0:LEFT_HALF] = jnp.zeros((SLAB, LEFT_HALF), LOW)
            pack[:, LEFT_HALF:] = handed[...]

        own_pack().start()

        @pl.loop(1, replicas)
        def _(step):
            pack_copy(step).start()

    def add(target, *sources):
        value = target[...].astype(F32)
        for source in sources:
            value = value + source[...].astype(F32)
        target[...] = value.astype(LOW)

    def landing(block):
        return blocks.at[8 + block, 0] if block < 4 else core_in.at[block - 4]

    def scatter(block, stage):
        run = blocks.at[part(block)]
        source, target, peer = (
            (run.at[:, :, 1 - core], landing(block), beside_core),
            (run.at[:, 1 - x, core, upper], one_a.at[block], beside_x),
            (run.at[1 - y, :, core, lower], one_b.at[block], beside_y),
            (run.at[1 - y, x, core, upper], two_a.at[block], beside_y),
            (run.at[y, 1 - x, core, lower], two_b.at[block], beside_x),
        )[stage]
        return remote(source, target, rs_send.at[block, stage], rs_recv.at[block, stage], peer)

    def to_line(block, step):
        side = 0 if step < 0 else 1
        return remote(
            blocks.at[part(block), y, x, core],
            line_in.at[block, side],
            z_send.at[block],
            z_recv.at[block, side],
            {"section": lax.rem(me + step + sections, sections)},
        )

    def to_group(block, step):
        return remote(
            blocks.at[part(block), y, x, core],
            group_in.at[block, step - 1],
            group_send.at[block, step - 1],
            group_recv.at[block, step - 1],
            {"dp": lax.rem(index + step * CUBE, replicas)},
        )

    def gather_back(block, stage):
        place = OWN[HOLDER[block]].index(block)
        run = blocks.at[part(block)]
        ref, peer = (
            (run.at[y, x, core, upper], beside_y),
            (run.at[y, x, core, lower], beside_x),
            (run.at[:, x, core, upper], beside_x),
            (run.at[y, :, core, lower], beside_y),
            (run.at[:, :, core], beside_core),
        )[stage]
        return remote(ref, ref, ag_send.at[place, stage], ag_recv.at[place, stage], peer)

    def write_out(block):
        place = OWN[HOLDER[block]].index(block)
        return pltpu.make_async_copy(
            blocks.at[part(block)], total.at[place], out_sem.at[place]
        )

    def reduce_core(block):
        scatter(block, 0).start()

    def reduce_one(block):
        scatter(block, 0).wait()
        arrived = landing(block)
        for yy in range(2):
            for xx in range(2):
                add(blocks.at[part(block), yy, xx, core], arrived.at[yy, xx])
        scatter(block, 1).start()
        scatter(block, 2).start()

    def reduce_two(block):
        run = blocks.at[part(block)]
        scatter(block, 1).wait()
        for yy in range(2):
            add(run.at[yy, x, core, upper], one_a.at[block, yy])
        scatter(block, 3).start()
        scatter(block, 2).wait()
        for xx in range(2):
            add(run.at[y, xx, core, lower], one_b.at[block, xx])
        scatter(block, 4).start()

    def reduce_three(block):
        run = blocks.at[part(block)]
        scatter(block, 3).wait()
        add(run.at[y, x, core, upper], two_a.at[block])
        scatter(block, 4).wait()
        add(run.at[y, x, core, lower], two_b.at[block])
        if groups > 1:
            for step in range(1, groups):
                to_group(block, step).start()
            for step in range(1, groups):
                to_group(block, step).wait()
            for step in range(1, groups):
                copy = pltpu.make_async_copy(group_in.at[block, step - 1], group_piece, group_load)
                copy.start()
                copy.wait()
                add(run.at[y, x, core], group_piece)
        reduce_line(0, block)

    def reduce_line(hop, block):
        holder = HOLDER[block]
        target = blocks.at[part(block), y, x, core]
        for section in range(sections):
            from_above = sections - 1 - section if section >= holder else -1
            from_below = section if section <= holder else -1
            if max(from_above, from_below) != hop:
                continue

            @pl.when(me == section)
            def _():
                if from_above > 0:
                    to_line(block, -1).wait_recv()
                    add(target, line_in.at[block, 0])
                if from_below > 0:
                    to_line(block, 1).wait_recv()
                    add(target, line_in.at[block, 1])
                if section != holder:
                    to_line(block, -1 if section > holder else 1).start()

    def spread_one(block):
        @pl.when(me == HOLDER[block])
        def _():
            gather_back(block, 0).start()
            gather_back(block, 1).start()

    def spread_two(block):
        @pl.when(me == HOLDER[block])
        def _():
            gather_back(block, 0).wait()
            gather_back(block, 2).start()
            gather_back(block, 1).wait()
            gather_back(block, 3).start()

    def spread_core(block):
        @pl.when(me == HOLDER[block])
        def _():
            gather_back(block, 2).wait()
            gather_back(block, 3).wait()
            gather_back(block, 4).start()

    def spread_done(block):
        @pl.when(me == HOLDER[block])
        def _():
            gather_back(block, 4).wait()
            write_out(block).start()

        @pl.when(me != HOLDER[block])
        def _():
            to_line(block, 1).wait_send()

    reduce_stages = (
        [reduce_one, reduce_two, reduce_three]
        + [partial(reduce_line, hop) for hop in range(1, sections)]
        + [spread_one, spread_two, spread_core, spread_done]
    )

    def reduce_tick(order, tick):
        for place, stage in enumerate(reduce_stages):
            if 0 <= tick - 1 - place < len(order):
                stage(order[tick - 1 - place])

    wave_one, wave_two = (8, 9, 10, 11, 4, 5, 6, 7), (3, 0, 1, 2)
    ticks_one = len(wave_one) + len(reduce_stages)
    ticks_two = len(wave_two) + len(reduce_stages)

    small[...] = jnp.zeros_like(small)
    for tick in range(GATHERED + 4):
        gather_tick(tick)
        if tick == 4:
            for step in range(1, sections):
                vector_copy(step).wait()
        if 4 <= tick < 7:
            project(tick - 4)
        if tick == 6:
            heads_forward(0)
        if tick == 7:
            heads_forward(1)
            attention_close()
            h1_slab[...] = lead_rows(h1)
            lead_start(H1, h1_slab, h1_leads, 1)
        if 8 <= tick < 12:
            inner_block(tick - 8)
        if 12 <= tick < 16:
            second_block(tick - 12)
        if tick == 15:
            mlp_close()
            h2_slab[...] = lead_rows(layer_out)
            lead_start(H2, h2_slab, h2_leads, 2)
            mlp_open_backward()

    for block in gather_order:
        gather_finish(block)

    step = 0
    for block in range(4):
        second_grad(block)
        reduce_core(8 + block)
        reduce_tick(wave_one, step)
        step += 1
    leads_first()
    for block in range(4):
        inner_grad(block)
        reduce_core(4 + block)
        reduce_tick(wave_one, step)
        step += 1
    leads_second()
    for _ in range(2):
        reduce_tick(wave_one, step)
        step += 1
    leads_third()
    reduce_tick(wave_one, step)
    step += 1
    leads_fourth()
    pl.semaphore_signal(credit, inc=1, device_id=beside_core, device_id_type=MESH)
    reduce_tick(wave_one, step)
    step += 1
    leads_close()
    attention_open_backward()
    out_grad()
    pl.semaphore_wait(credit, 1)
    reduce_core(3)
    reduce_tick(wave_one, step)
    step += 1
    heads_backward(0)
    heads_backward(1)
    later = 1
    for block in range(3):
        project_grad(block)
        reduce_core(block)
        reduce_tick(wave_one, step)
        reduce_tick(wave_two, later)
        step += 1
        later += 1

    def small_copy(step):
        return remote(
            small, small_all.at[index], small_send.at[step], small_recv.at[step], replica(step)
        )

    def sum_copy(step):
        return remote(
            small_sum, smalls.at[me], sum_send.at[step], sum_recv.at[step], others[step - 1]
        )

    def own_sum():
        return pltpu.make_async_copy(small_sum, smalls.at[me], sum_send.at[0])

    @pl.loop(1, replicas)
    def _(step):
        small_copy(step).start()

    small_all[index] = small[...]
    for block in range(3):
        tokens_back(block)
        if step < ticks_one:
            reduce_tick(wave_one, step)
            step += 1
        reduce_tick(wave_two, later)
        later += 1
    grad_tokens[...] = summed[...].astype(LOW)

    @pl.loop(1, replicas)
    def _(step):
        small_copy(step).wait()

    small_sum[...] = jnp.sum(small_all[...], axis=0)
    for place in range(1, sections):
        sum_copy(place).start()
    own_sum().start()
    while step < ticks_one or later < ticks_two:
        if step < ticks_one:
            reduce_tick(wave_one, step)
            step += 1
        if later < ticks_two:
            reduce_tick(wave_two, later)
            later += 1

    for place in range(1, sections):
        sum_copy(place).wait()
    own_sum().wait()
    own_pack().wait()

    @pl.loop(1, replicas)
    def _(step):
        pack_copy(step).wait()

    for holder in (0, 1):

        @pl.when(me == holder)
        def _():
            for block in OWN[holder]:
                write_out(block).wait()

    for kind, slab, target, reader in (
        (COT, cot_slab, cot_leads, 3),
        (H1, h1_slab, h1_leads, 1),
        (H2, h2_slab, h2_leads, 2),
    ):

        @pl.when(me != reader)
        def _():
            lead_copy(kind, slab, target, reader).wait_send()

    @pl.when(me == 1)
    def _():
        for place in range(1, sections):
            spread_copy(GRAD1, lead_grad1, place).wait_send()
        hop_copy(HAND, handed, -1).wait_send()

    @pl.when(me == 2)
    def _():
        hop_copy(THIRD, lead_third, 1).wait_send()
        hop_copy(GRAD2, lead_grad2, -1).wait_send()

    @pl.when(me == 3)
    def _():
        for place in range(1, sections):
            spread_copy(FOURTH, lead_fourth, place).wait_send()
        hop_copy(GRAD3, lead_grad3, -1).wait_send()
        hop_copy(HAND, handed, -1).wait_send()


def run_layers(sections, replicas, tokens, cotangent, code, vector, wide, half):
    groups = replicas // CUBE
    rows = tokens.shape[0]
    block = (2, 2, 2, PIECE, D)
    reduced_groups = max(groups - 1, 1)
    in_vmem = pl.BlockSpec(memory_space=pltpu.VMEM)
    anywhere = pl.BlockSpec(memory_space=pl.ANY)
    slab = pltpu.VMEM((SLAB, D), LOW)
    leads = pltpu.VMEM((sections, SLAB, D), LOW)
    return pl.pallas_call(
        partial(layer_kernel, sections, replicas),
        out_shape=(
            jax.ShapeDtypeStruct(tokens.shape, LOW),
            jax.ShapeDtypeStruct(tokens.shape, LOW),
            jax.ShapeDtypeStruct((OWNED,) + block, LOW),
            jax.ShapeDtypeStruct((replicas, SLAB, PACK), LOW),
            jax.ShapeDtypeStruct((sections,) + vector.shape, F32),
            jax.ShapeDtypeStruct(
                (REDUCED if groups > 1 else 1, reduced_groups, PIECE, D), LOW
            ),
        ),
        in_specs=[in_vmem] * 4 + [anywhere] * 2,
        out_specs=[in_vmem] * 2 + [anywhere] * 4,
        scratch_shapes=[
            pltpu.VMEM((REDUCED + 8,) + block, LOW),
            pltpu.VMEM((8,) + block, LOW),
            pltpu.VMEM((8, 2, 2, PIECE, D), LOW),
            pltpu.VMEM((REDUCED, 2, HALF, D), LOW),
            pltpu.VMEM((REDUCED, 2, HALF, D), LOW),
            pltpu.VMEM((REDUCED, HALF, D), LOW),
            pltpu.VMEM((REDUCED, HALF, D), LOW),
            pltpu.VMEM((REDUCED, 2, PIECE, D), LOW),
            pltpu.VMEM((sections,) + vector.shape, F32),
            pltpu.VMEM((rows, 3 * D), LOW),
            pltpu.VMEM((2, PAIRS, 2, rows // 2, rows // 2), F32),
            pltpu.VMEM((rows, D), LOW),
            pltpu.VMEM((rows, D), LOW),
            pltpu.VMEM((rows, D), F32),
            pltpu.VMEM((rows, 128), F32),
            pltpu.VMEM((rows, D), F32),
            pltpu.VMEM((rows, 4 * D), LOW),
            pltpu.VMEM((rows, 4 * D), F32),
            pltpu.VMEM((rows, D), F32),
            pltpu.VMEM((rows, 128), F32),
            pltpu.VMEM((rows, D), F32),
            pltpu.VMEM((rows, D), LOW),
            slab, slab, slab, leads, leads, leads,
            slab, slab, slab, slab, slab,
            pltpu.VMEM((SLAB, 3 * D), LOW),
            pltpu.VMEM((SLAB, 3 * D), LOW),
            pltpu.VMEM((PAIRS, 2, SLAB, SLAB), F32),
            slab,
            pltpu.VMEM((SLAB, D), F32),
            pltpu.VMEM((SLAB, 128), F32),
            pltpu.VMEM((SLAB, 4 * D), LOW),
            pltpu.VMEM((SLAB, 4 * D), F32),
            pltpu.VMEM((SLAB, PACK), LOW),
            pltpu.VMEM(vector.shape, F32),
            pltpu.VMEM((replicas,) + vector.shape, F32),
            pltpu.VMEM(vector.shape, F32),
            pltpu.VMEM((PIECE, D), LOW),
            DMA((GATHERED, 2)),
            DMA((GATHERED,)),
            DMA((GATHERED, 5)),
            DMA((GATHERED, 5)),
            DMA((GATHERED,)),
            DMA((REDUCED, 5)),
            DMA((REDUCED, 5)),
            DMA((REDUCED,)),
            DMA((REDUCED, 2)),
            DMA((REDUCED, reduced_groups)),
            DMA((REDUCED, reduced_groups)),
            DMA,
            DMA((OWNED, 5)),
            DMA((OWNED, 5)),
            DMA((OWNED,)),
            DMA((replicas,)),
            DMA((replicas,)),
            DMA((replicas,)),
            DMA((replicas,)),
            DMA((sections,)),
            DMA((sections,)),
            DMA((sections,)),
            DMA((sections,)),
            DMA((3,)),
            DMA((3, sections)),
            DMA((2, sections)),
            DMA((2,)),
            DMA((4,)),
            DMA((4,)),
            pltpu.SemaphoreType.REGULAR,
        ],
        compiler_params=pltpu.CompilerParams(
            collective_id=0, has_side_effects=True, vmem_limit_bytes=VMEM_BYTES
        ),
    )(tokens, cotangent, code, vector, wide, half)


VMEM_BYTES = 62 * 1024 * 1024


def close_kernel(total, packs, smalls, wide_out, half_out, gain_out, bias_out):
    me = lax.axis_index("section")
    step = pl.program_id(0)
    near = me < 2
    packed = packs[...].reshape(-1, PACK)
    summed = jnp.where(near, total[0].reshape(D, D).astype(F32), 0.0)

    def wide_step(block):
        @pl.when(step == block)
        def _():
            left = packed[:, 0:D] if block < 3 else packed[:, LEFT_OUT:RIGHT]
            right = packed[:, RIGHT + block * D : RIGHT + (block + 1) * D]
            wide_out[0] = summed + outer(left, right)

    def half_step(block):
        @pl.when(step == 4 + block)
        def _():
            left = packed[:, LEFT_HALF + block * D : LEFT_HALF + (block + 1) * D]
            half_out[0] = summed + outer(left, packed[:, RIGHT_HALF:])

    for block in range(4):
        wide_step(block)
    for block in range(2):
        half_step(block)

    @pl.when(step == 0)
    def _():
        every = jnp.sum(smalls[...], axis=0)
        mine = smalls[me]
        for row, out in ((0, gain_out), (1, bias_out)):
            value = jnp.where(me == 0, every[row : row + 1], every[2 + row : 3 + row])
            value = jnp.where(near, value, 0.0) + mine[4 + row : 5 + row]
            out[...] = value


def close(total, packs, smalls):
    whole = lambda array: pl.BlockSpec(array.shape, lambda step: (0,) * array.ndim)
    return pl.pallas_call(
        close_kernel,
        grid=(OWNED,),
        out_shape=(
            jax.ShapeDtypeStruct((1, D, 4 * D), F32),
            jax.ShapeDtypeStruct((1, 2 * D, D), F32),
            jax.ShapeDtypeStruct((1, D), F32),
            jax.ShapeDtypeStruct((1, D), F32),
        ),
        in_specs=[
            pl.BlockSpec((1,) + total.shape[1:], lambda step: (step, 0, 0, 0, 0, 0)),
            whole(packs),
            whole(smalls),
        ],
        out_specs=[
            pl.BlockSpec((1, D, D), lambda step: (0, 0, jnp.minimum(step, 3))),
            pl.BlockSpec((1, D, D), lambda step: (0, jnp.maximum(step - 4, 0), 0)),
            pl.BlockSpec((1, D), lambda step: (0, 0)),
            pl.BlockSpec((1, D), lambda step: (0, 0)),
        ],
        compiler_params=pltpu.CompilerParams(vmem_limit_bytes=VMEM_BYTES),
    )(total, packs, smalls)


def on_device(tokens, cotangent, seg_doc, wide_in, half_out, norm_gain, norm_bias):
    sections = lax.axis_size("section")
    replicas = lax.axis_size("dp")
    vector = jnp.concatenate([norm_gain, norm_bias, jnp.zeros((6, D), F32)], axis=0)
    doc = jnp.concatenate([seg_doc.reshape(-1), jnp.zeros((SLAB - seg_doc.size,), jnp.int32)])
    owner = jnp.arange(SLAB) // seg_doc.shape[1]
    same = owner[:, None] == owner[None, :]
    code = jnp.where(same, jnp.where(doc[:, None] == doc[None, :], 2.0, 1.0), 0.0)
    wide = wide_in.reshape(2, 2, 2, PIECE, 4 * D)
    half = half_out.reshape(2, 2, 2, 2, PIECE, D)
    layer_out, grad_tokens, total, packs, smalls, _ = run_layers(
        sections, replicas, tokens, cotangent, code.astype(F32), vector, wide, half
    )
    return (layer_out, grad_tokens) + tuple(close(total, packs, smalls))


def solution(mesh):
    placed = (
        P(("dp", "section"), None),
        P(("dp", "section"), None),
        P("dp", None),
        P("section", None, None),
        P("section", None, None),
        P("section", None),
        P("section", None),
    )
    return jax.shard_map(
        on_device,
        mesh=mesh,
        in_specs=placed,
        out_specs=(
            P(("dp", "section"), None),
            P(("dp", "section"), None),
            P("section", None, None),
            P("section", None, None),
            P("section", None),
            P("section", None),
        ),
        check_vma=False,
    )
```

time: 1130 us -> 281 us (0.25)
  waiting for transfers between devices: 471 us -> 0 us
  Pallas kernels: 0 us -> 275 us
  local copies, waits for them, and re-layouts: 179 us -> 2.43 us
  other arithmetic: 148 us -> 2.06 us
  matrix products: 133 us -> 0 us
  loops' own time: 117 us -> 0 us
  starting transfers between devices: 47.2 us -> 0 us
  between operations: 15.1 us -> 0.67 us
  blocking collectives: 13.7 us -> 0 us
    pallas_call x0 -> x2, Pallas kernels: none -> 275 us  [the longest x1 263 us: run_layers(): pl.pallas_call(partial(layer_kernel, sections, replicas), out_shape=(jax....]
    ppermute x14 -> x0, waiting for transfers between devices: 213 us -> none  [passed_along(): lax.ppermute(value, axis, [(source, source + steps) for source in range(l...]
    psum x1 -> x0, waiting for transfers between devices: 199 us -> none  [on_device(): lax.psum((sum_first, sum_second, sum_gain, sum_bias), 'dp')]
    another operation x14 -> x0, loops' own time: 117 us -> none  [the longest x7 75.6 us: on_device(): lax.switch(chosen, backward_fns, kept_inputs[slot], grad_out, seg_doc[slot])]
    dot_general x56 -> x0, matrix products: 112 us -> none  [the longest x8 28.1 us: attention_forward(): jnp.dot(hidden, weights[:, :3 * D], preferred_element_type=jnp.float32)]
    all_gather x2 -> x0, waiting for transfers between devices: 52.4 us -> none  [the longest x1 52.4 us: on_device(): lax.all_gather(tokens, 'section', axis=0, tiled=True)]
    broadcast_in_dim x12 -> x1, local copies, waits for them, and re-layouts: 44.1 us -> 0.01 us  [on_device(): jnp.zeros((6, D), F32)]
    cond x166 -> x0, local copies, waits for them, and re-layouts: 42.8 us -> none  [the longest x4 38.4 us: on_device(): lax.switch(chosen, backward_fns, kept_inputs[slot], grad_out, seg_doc[slot])]
  transfers between devices with their start and end apart: 19 -> 0, of which waited for: 17 -> 0; matrix products, arithmetic and copies ran while one was open for 7% -> 0% of each run, Pallas kernels for 0% -> 0%
where the time goes in v2:
time: 281 us; the launch traced here: 280 us
  Pallas kernels  275 us (98%)
    pallas_call x1, Pallas kernels, run_layers(): pl.pallas_call(partial(layer_kernel, sections, replicas), out_shape=(jax....  263 us
    pallas_call x1, Pallas kernels, close(): pl.pallas_call(close_kernel, grid=(OWNED,), out_shape=(jax.ShapeDtypeStru...  12.3 us

profile of v2, /device:TPU:0, one launch (start us, length us, event | category | flops | bytes accessed | tf_op | source)
XLA Modules:
  0.0 280.3 jit_solution(6503729470816686256)
XLA Ops:
  0.6 0.1 pad.3.clone
  0.7 0.8 copy.14
  1.5 0.1 reshape.49
  1.6 0.7 select_select_fusion.code
  2.3 1.4 maximum_maximum_fusion.vector
  3.6 262.8 %shard_map.118 = (bf16[256,768]{1,0:T(8,128)(2,1)}, bf16[256,768]{1,0:T(8,128)(2,1)}, bf16[6,2,2,2,96,768]{5,4,3,2,1,0:T(8,128)(2,1)}, bf16[8,16,6912]{2,1,0:T(8...) custom-call(bf16[256,768]{1,0:T(8,128)(2,1)} %tokens.1, bf16[256,768]{1,0:T(8,128)(2,1)} %cotangent.1, ...), custom_call_target="tpu_custom_call" | custom-call | tf_op jit(solution)/shard_map/pallas_call | solution.py:1060
  266.5 0.0 copy-start.1
  266.5 0.0 copy-start
  266.5 12.3 %shard_map.119 = (f32[1,768,3072]{2,1,0:T(8,128)}, f32[1,1536,768]{2,1,0:T(8,128)}, f32[1,768]{1,0:T(1,128)}, f32[1,768]{1,0:T(1,128)}) custom-call(bf16[6,2,2,2,96,768]{5,4,3,2,1,0:T(8,128)(2,1)} %get-tuple-element.17.total, bf16[8,16,6912]{2,1,0:T(8,128)(2,1)} %get-tuple-element.18.packs, f32[4,8,768]{2,1,0:T(8,128)} %get-tuple-element.19.smalls), custom_call_target="tpu_custom_call" | custom-call | tf_op jit(solution)/shard_map/pallas_call | solution.py:1189
  278.8 0.0 copy-done.1
  278.8 0.7 copy.17
  279.6 0.0 copy-done
  279.6 0.7 copy.18
  (3 shorter events, 0.0 us)
Async XLA Ops:
  266.5 12.3 %copy-start.1 = (bf16[256,768]{1,0:T(8,128)(2,1)S(1)}, bf16[256,768]{1,0:T(8,128)(2,1)}, u32[]{:S(2)}) copy-start(bf16[256,768]{1,0:T(8,128)(2,1)} %get-tuple-element.30) | copy-start | bytes 1179652
  266.5 13.1 %copy-start = (bf16[256,768]{1,0:T(8,128)(2,1)S(1)}, bf16[256,768]{1,0:T(8,128)(2,1)}, u32[]{:S(2)}) copy-start(bf16[256,768]{1,0:T(8,128)(2,1)} %get-tuple-element.31) | copy-start | bytes 1179652
